TPU v7x, 256 devices: a whole 4x4x8 slice. The times are simulated.
256 devices in a mesh: ctx: 64 (over y, x_hi, z), tp: 4 (over x_lo, core).
Axes of the slice: x: 4 (x_hi: 2, x_lo: 2; x = x_hi * 2 + x_lo), y: 4, z: 8, core: 2. Of those that a mesh axis runs over, the one named last changes fastest.
Arguments:
- projected: bfloat16 [32768, 3, 4096], P('ctx', None, 'tp'), may hold values from -6 to 6
- short_taps: float32 [3, 3, 4096], P(None, None, 'tp'), may hold values from -3.5 to 3.5
- filter_taps: float32 [4096, 128], P('tp'), may hold values from -0.75 to 0.75
- decay_rates: float32 [4096], P('tp'), may hold values from 0.002 to 0.1
- bypass_gain: float32 [4096], P('tp'), may hold values from -5 to 5
- out_weight: bfloat16 [4096, 8192], P('tp', 'ctx'), may hold values from -0.09375 to 0.09375
Outputs:
- block_out: bfloat16 [32768, 8192], P(('ctx', 'tp'))
All inputs are finite; a program needn't handle non-finite values.
Results may differ from a plain program's by a relative error of at most 0.013.
Values may be sent and summed in bfloat16 or wider, within the bound.
No kernel may reach another device: no remote copies, remote signals or barrier semaphores. Data moves between devices by JAX's collectives and lax.ppermute only.
A program may use at most 192 MiB of HBM per device.

v0:
```python
import jax
import jax.numpy as jnp
from jax import lax
from jax.sharding import PartitionSpec as P


def shifted(value, axis, steps):
    count = lax.axis_size(axis)
    leading, last = (max(0, -steps), min(count, count - steps))
    return lax.ppermute(value, axis, [(source, source + steps) for source in range(leading, last)])


def featurize(raw_rows, short_taps, row_total):
    running = short_taps[0] * raw_rows[2 : 2 + row_total].astype(jnp.float32)
    running = running + short_taps[1] * raw_rows[1 : 1 + row_total].astype(jnp.float32)
    running = running + short_taps[2] * raw_rows[0:row_total].astype(jnp.float32)
    return running.astype(jnp.bfloat16)


def multiply_streams(featured):
    return (featured[:, 1].astype(jnp.float32) * featured[:, 2].astype(jnp.float32)).astype(
        jnp.bfloat16
    )


def causal_filter(extended_products, filter_bank):
    kernel = jnp.flip(filter_bank, axis=1).T[:, None, :]
    result = lax.conv_general_dilated(
        extended_products[None],
        kernel,
        (1,),
        "VALID",
        dimension_numbers=("NWC", "WIO", "NWC"),
        feature_group_count=extended_products.shape[1],
        preferred_element_type=jnp.float32,
    )
    return result[0]


def on_device(projected, short_taps, filter_taps, decay_rates, bypass_gain, out_weight):
    rows_here = projected.shape[0]
    tap_count = filter_taps.shape[1]
    tap_lags = jnp.arange(tap_count).astype(jnp.float32)
    filter_bank = (filter_taps * jnp.exp(-decay_rates[:, None] * tap_lags[None, :])).astype(
        jnp.bfloat16
    )
    earlier_rows = shifted(projected[rows_here - tap_count - 1 :], "ctx", 1)
    extended = jnp.concatenate([earlier_rows, projected], axis=0)
    featured_all = featurize(extended, short_taps, rows_here + tap_count - 1)
    product_all = multiply_streams(featured_all)
    query_rows = featured_all[tap_count - 1 :, 0]
    product_here = product_all[tap_count - 1 :]
    long_part = causal_filter(product_all, filter_bank)
    gated = (
        query_rows.astype(jnp.float32)
        * (long_part + bypass_gain * product_here.astype(jnp.float32))
    ).astype(jnp.bfloat16)
    partial_value = jnp.dot(
        gated,
        lax.all_gather(out_weight, "ctx", axis=1, tiled=True),
        preferred_element_type=jnp.float32,
    )
    summed = lax.psum_scatter(
        partial_value.astype(jnp.bfloat16), "tp", scatter_dimension=0, tiled=True
    )
    return summed


def solution(mesh):
    return jax.shard_map(
        on_device,
        mesh=mesh,
        in_specs=(
            P("ctx", None, "tp"),
            P(None, None, "tp"),
            P("tp", None),
            P("tp"),
            P("tp"),
            P("tp", "ctx"),
        ),
        out_specs=P(("ctx", "tp"), None),
        check_vma=False,
    )
```

profile of v0, /device:TPU:1, one launch (start us, length us, event | category | flops | bytes accessed | tf_op | source)
XLA Modules:
  0.0 380.4 jit_solution(6552322254034345371)
XLA Ops:
  6.5 0.0 all-gather.2.cloned.1.call-start
  6.5 0.7 all-gather.2.cloned.1.call-update
  7.3 0.0 reduce-scatter.2.cloned.1.call-start
  7.3 2.4 slice.35
  9.7 5.3 %collective-permute-start = (bf16[129,3,1024]{2,0,1:T(8,128)(2,1)}, bf16[129,3,1024]{2,0,1:T(8,128)(2,1)}, u32[]{:S(2)}, u32[]{:S(2)}) collective-permute-start(bf16[129,3,1024]{2,0,1:T(8,128)(2,1)} %slice.35), channel_id=1, source_target_pairs={{0,4},{4,8},{8,12},{12,16},{16,20},{20,24},{24,28},{28,32},{32,36}... | collective-permute-start | bytes 2377736 | tf_op jit(solution)/shard_map/ppermute | solution.py:10
  15.0 0.7 neg.4
  15.7 2.0 multiply_convert_fusion.1
  17.7 3.5 rev.4
  21.2 1.2 copy.8
  22.3 0.0 copy-done.4
  22.4 9.3 %collective-permute-done = bf16[129,3,1024]{2,0,1:T(8,128)(2,1)} collective-permute-done((bf16[129,3,1024]{2,0,1:T(8,128)(2,1)}, bf16[129,3,1024]{2,0,1:T(8,128)(2,1)}, u32[]{:S(2)}, u32[]{:S(2)}) %collective-permute-start) | collective-permute-done | bytes 792608 | tf_op jit(solution)/shard_map/ppermute | solution.py:10
  31.7 4.8 %add_convert_fusion = bf16[639,3,1024]{2,0,1:T(8,128)(2,1)S(1)} fusion(bf16[129,3,1024]{2,0,1:T(8,128)(2,1)} %collective-permute-done, bf16[512,3,1024]{2,0,1:T(8,128)(2,1)S(1)} %copy-done.1, f32[3,1024]{1,0:T(4,128)S(1)} %get-tuple-element.6, f32[3,1024]{1,0:T(4,128)S(1)} %get-tuple-element.7, f32[3,1024]{1,0:T(4,128)S(1)} %get-tuple-element.5), kind=kLoop, calls=%fused_computation.1 | loop fusion | flops 35334144 | bytes 7901184 | tf_op jit(solution)/shard_map/convert_element_type | solution.py:17
  36.4 0.0 copy-start
  36.4 0.0 copy-start.3
  36.5 0.5 fusion.10
  37.0 1.3 copy-done
  38.3 1.6 multiply_convert_fusion
  39.9 0.0 copy-done.3
  39.9 31.0 %fusion.2 = f32[1,512,1024]{2,0,1:T(1,128)S(1)} fusion(bf16[128,1,1024]{2,1,0:T(2,128)(2,1)S(1)} %copy-done.3, bf16[1,639,1024]{2,1,0:T(8,128)(2,1)S(1)} %fusion.10), kind=kOutput, calls=%fused_computation.8 | convolution fusion | flops 134217728 | bytes 3667968 | tf_op jit(solution)/shard_map/conv_general_dilated | solution.py:28
  70.9 206.5 %all-gather.2.cloned.1.call-done = bf16[1024,8192]{1,0:T(8,128)(2,1)} async-done(((bf16[1024,128]{1,0:T(8,128)(2,1)}), bf16[1024,8192]{1,0:T(8,128)(2,1)}) %all-gather.2.cloned.1.call-update) | async-done | bytes 16777232 | tf_op jit(solution)/shard_map/all_gather | solution.py:60
  277.4 0.0 copy-done.5
  277.4 15.2 %convolution_convert_fusion = bf16[512,8192]{1,0:T(8,128)(2,1)} fusion(bf16[1024,8192]{1,0:T(8,128)(2,1)} %all-gather.2.cloned.1.call-done, f32[1,512,1024]{2,0,1:T(1,128)S(1)} %fusion.2, bf16[639,1,1024]{2,0,1:T(8,128)(2,1)S(1)} %copy-done.2, bf16[639,3,1024]{2,0,1:T(8,128)(2,1)} %copy-done, f32[1024]{0:T(1024)S(1)} %copy-done.5), kind=kOutput, calls=%fused_computation | convolution fusion | flops 8597274624 | bytes 29364224 | tf_op jit(solution)/shard_map/dot_general | solution.py:58
  292.6 0.0 reduce-scatter.2.cloned.1.call-update
  292.7 80.9 %reduce-scatter.2.cloned.1.call-done = bf16[128,8192]{1,0:T(8,128)(2,1)} async-done(((bf16[512,8192]{1,0:T(8,128)(2,1)}), bf16[128,8192]{1,0:T(8,128)(2,1)}) %reduce-scatter.2.cloned.1.call-update) | async-done | bytes 2097168 | tf_op jit(solution)/shard_map/reduce_scatter | solution.py:63
  (8 shorter events, 0.0 us)
Async XLA Ops:
  6.5 25.1 %copy-start.1 = (bf16[512,3,1024]{2,0,1:T(8,128)(2,1)S(1)}, bf16[512,3,1024]{2,0,1:T(8,128)(2,1)}, u32[]{:S(2)}) copy-start(bf16[512,3,1024]{2,0,1:T(8,128)(2,1)} %param.6) | copy-start | bytes 9437188
  6.5 15.8 %copy-start.4 = (f32[3,3,1024]{2,1,0:T(4,128)S(1)}, f32[3,3,1024]{2,1,0:T(4,128)}, u32[]{:S(2)}) copy-start(f32[3,3,1024]{2,1,0:T(4,128)} %param.7) | copy-start | bytes 110596
  6.5 270.9 %all-gather.2.cloned.1.call-start = ((), (), s32[]{:S(2)}) async-start(), calls=%async_computation.1 | async-start | bytes 17039360 | tf_op jit(solution)/shard_map/all_gather | solution.py:60
  7.3 366.3 %reduce-scatter.2.cloned.1.call-start = ((), (), s32[]{:S(2)}) async-start(), calls=%async_computation.2 | async-start | bytes 10485760 | tf_op jit(solution)/shard_map/reduce_scatter | solution.py:63
  9.7 21.9 %collective-permute-start = (bf16[129,3,1024]{2,0,1:T(8,128)(2,1)}, bf16[129,3,1024]{2,0,1:T(8,128)(2,1)}, u32[]{:S(2)}, u32[]{:S(2)}) collective-permute-start(bf16[129,3,1024]{2,0,1:T(8,128)(2,1)} %slice.35), channel_id=1, source_target_pairs={{0,4},{4,8},{8,12},{12,16},{16,20},{20,24},{24,28},{28,32},{32,36}... | collective-permute-start | bytes 2377736 | tf_op jit(solution)/shard_map/ppermute | solution.py:10
  36.4 1.9 copy-start
  36.4 3.5 copy-start.3
  39.9 237.5 %copy-start.2 = (bf16[639,1,1024]{2,0,1:T(8,128)(2,1)S(1)}, bf16[639,1,1024]{2,0,1:T(8,128)(2,1)}, u32[]{:S(2)}) copy-start(bf16[639,1,1024]{2,0,1:T(8,128)(2,1)} %multiply_convert_fusion) | copy-start | bytes 3926020
  39.9 237.5 %copy-start.5 = (f32[1024]{0:T(1024)S(1)}, f32[1024]{0:T(1024)}, u32[]{:S(2)}) copy-start(f32[1024]{0:T(1024)} %param.10) | copy-start | bytes 12292
Sparse Core Ops, SparseCore 0:
  10.8 266.6 all-gather.1
  292.8 80.7 reduce-scatter.1
where the time goes:
time: 381 us; the launch traced here: 380 us
  waiting for transfers between devices  297 us (78%)
  matrix products  46.2 us (12%)
  between operations  13.5 us (4%)
  other arithmetic  9.56 us (3%)
  local copies, waits for them, and re-layouts  8.4 us (2%)
  starting transfers between devices  5.33 us (1%)
    all_gather x1, waiting for transfers between devices, on_device(): lax.all_gather(out_weight, 'ctx', axis=1, tiled=True)  207 us
    reduce_scatter x1, waiting for transfers between devices, on_device(): lax.psum_scatter(partial_value.astype(jnp.bfloat16), 'tp', scatter_dimens...  80.9 us
    conv_general_dilated x1, matrix products, causal_filter(): lax.conv_general_dilated(extended_products[None], kernel, (1,), 'VALID',...  31 us
    dot_general x1, matrix products, on_device(): jnp.dot(gated, lax.all_gather(out_weight, 'ctx', axis=1, tiled=True), pre...  15.2 us
    ppermute x1, waiting for transfers between devices, shifted(): lax.ppermute(value, axis, [(source, source + steps) for source in range(l...  9.31 us
  transfers between devices with their start and end apart: 3, of which 3 were waited for; matrix products, arithmetic and copies ran while one was open for 13% of the time, Pallas kernels for 0%

commit v1 on v0

v1 whole, which is shorter than its diff:
```python
import functools

import jax
import jax.numpy as jnp
import ml_dtypes
import numpy as np
from jax import lax
from jax.experimental import pallas as pl
from jax.experimental.pallas import tpu as pltpu
from jax.sharding import Mesh
from jax.sharding import PartitionSpec as P

TOK = 512
CH = 1024
TAPS = 128
WIN = 256
LANES = 256
CELL = ("xh", "xl", "c")
F32, BF16 = jnp.float32, jnp.bfloat16


def two_halves(matrix):
    high = matrix.astype(ml_dtypes.bfloat16)
    low = (matrix - high.astype(np.float64)).astype(ml_dtypes.bfloat16)
    return high, low


@functools.lru_cache(maxsize=None)
def transform_matrices():
    at = np.arange(WIN)
    half = WIN // 2
    angle = 2 * np.pi * (np.outer(np.arange(half), at) % WIN) / WIN
    sine = -np.sin(angle)
    sine[0] = np.cos(np.pi * at)
    forward = np.concatenate([np.cos(angle), sine])
    scale = np.where(np.arange(half) == 0, 1.0, 2.0)[:, None] / WIN
    scale_im = np.where(np.arange(half) == 0, 1.0, 2.0)[:, None] / WIN
    inverse = np.concatenate([np.cos(angle) * scale, sine * scale_im]).T[half:]
    fh, fl = two_halves(forward)
    ih, il = two_halves(inverse)
    return np.concatenate([fh, fl]), np.concatenate([ih, ih, il], axis=1)


def rolled(x, steps):
    return pltpu.roll(x, steps % x.shape[0], 0)


def featurize(rows, taps, count):
    lead = rows.shape[0] - count
    one = rolled(rows, 1)[lead:]
    two = rolled(rows, 2)[lead:]
    return (taps[0] * rows[lead:] + taps[1] * one + taps[2] * two).astype(BF16)


def tail_kernel(x_ref, taps_ref, out_ref):
    start = TOK - TAPS - 16
    streams = []
    raw = []
    for s in range(3):
        rows = x_ref[s, start:TOK, :].astype(F32)
        raw.append(rows[-8:])
        if s:
            taps = [taps_ref[j, s : s + 1, :] for j in range(3)]
            streams.append(featurize(rows, taps, TAPS).astype(F32))
    out_ref[:TAPS, :] = (streams[0] * streams[1]).astype(BF16)
    row = lax.broadcasted_iota(jnp.int32, raw[0].shape, 0)
    packed = jnp.where(row < 2, rolled(raw[0], 2), jnp.where(row < 4, rolled(raw[1], 4), rolled(raw[2], 6)))
    out_ref[TAPS:, :] = jnp.concatenate([packed, jnp.zeros_like(packed)], axis=0).astype(BF16)


def tail_rows(x, taps):
    return pl.pallas_call(
        tail_kernel,
        grid=(2,),
        in_specs=[
            pl.BlockSpec((3, TOK, CH // 2), lambda i: (0, 0, i)),
            pl.BlockSpec((3, 3, CH // 2), lambda i: (0, 0, i)),
        ],
        out_specs=pl.BlockSpec((TAPS + 16, CH // 2), lambda i: (0, i)),
        out_shape=jax.ShapeDtypeStruct((TAPS + 16, CH), BF16),
        compiler_params=pltpu.CompilerParams(vmem_limit_bytes=32 << 20),
        cost_estimate=pl.CostEstimate(flops=4 * TAPS * CH, bytes_accessed=3 << 20, transcendentals=0),
    )(x, taps)


def mixer_kernel(x_ref, halo_ref, taps_ref, filt_ref, rate_ref, gain_ref, fwd_ref, inv_ref, out_ref, prod, query):
    dot = functools.partial(lax.dot_general, preferred_element_type=F32)
    plain = (((1,), (0,)), ((), ()))
    half = WIN // 2

    lag = lax.broadcasted_iota(jnp.int32, (LANES, TAPS), 1).astype(F32)
    bank = (filt_ref[...] * jnp.exp(-rate_ref[...] * lag)).astype(BF16)
    both = dot(fwd_ref[:, :half], bank, (((1,), (1,)), ((), ())))
    spectrum = both[:WIN] + both[WIN:]
    h_re, h_im = spectrum[:half], spectrum[half:]
    first = lax.broadcasted_iota(jnp.int32, h_re.shape, 0) == 0
    h_last = jnp.where(first, h_im, h_re)
    h_im = jnp.where(first, 0.0, h_im)

    prod[:TAPS] = halo_ref[:TAPS]
    raw = halo_ref[TAPS:].astype(F32)[:8]
    for b in range(TOK // TAPS):
        made = []
        for s in range(3):
            taps = [taps_ref[j, s : s + 1, :] for j in range(3)]
            if b:
                rows = x_ref[s, b * TAPS - 16 : (b + 1) * TAPS, :].astype(F32)
            else:
                rows = jnp.concatenate([rolled(raw, 6 - 2 * s), x_ref[s, :TAPS, :].astype(F32)], axis=0)
            made.append(featurize(rows, taps, TAPS))
        query[b * TAPS : (b + 1) * TAPS] = made[0]
        prod[(b + 1) * TAPS : (b + 2) * TAPS] = (made[1].astype(F32) * made[2].astype(F32)).astype(BF16)

    for b in range(TOK // TAPS):
        both = dot(fwd_ref[...], prod[b * TAPS : b * TAPS + WIN], plain)
        spectrum = both[:WIN] + both[WIN:]
        re, im = spectrum[:half], spectrum[half:]
        y = jnp.concatenate([re * h_re - im * h_im, re * h_im + im * h_last], axis=0)
        high = y.astype(BF16)
        low = (y - high.astype(F32)).astype(BF16)
        long_part = dot(inv_ref[...], jnp.concatenate([high, low, high], axis=0), plain)
        here = prod[(b + 1) * TAPS : (b + 2) * TAPS].astype(F32)
        q = query[b * TAPS : (b + 1) * TAPS].astype(F32)
        out_ref[b * TAPS : (b + 1) * TAPS, :] = (q * (long_part + gain_ref[...] * here)).astype(BF16)


def mixer(x, halo, taps, filt, rate, gain):
    forward, inverse = transform_matrices()
    steps = CH // LANES
    return pl.pallas_call(
        mixer_kernel,
        grid=(steps,),
        in_specs=[
            pl.BlockSpec((3, TOK, LANES), lambda i: (0, 0, i)),
            pl.BlockSpec((TAPS + 16, LANES), lambda i: (0, i)),
            pl.BlockSpec((3, 3, LANES), lambda i: (0, 0, i)),
            pl.BlockSpec((LANES, TAPS), lambda i: (i, 0)),
            pl.BlockSpec((LANES, 1), lambda i: (i, 0)),
            pl.BlockSpec((1, LANES), lambda i: (0, i)),
            pl.BlockSpec(forward.shape, lambda i: (0, 0)),
            pl.BlockSpec(inverse.shape, lambda i: (0, 0)),
        ],
        out_specs=pl.BlockSpec((TOK, LANES), lambda i: (0, i)),
        out_shape=jax.ShapeDtypeStruct((TOK, CH), BF16),
        scratch_shapes=[
            pltpu.VMEM((TOK + TAPS, LANES), BF16),
            pltpu.VMEM((TOK, LANES), BF16),
        ],
        compiler_params=pltpu.CompilerParams(vmem_limit_bytes=32 << 20),
        cost_estimate=pl.CostEstimate(flops=2 * 900 * 10**6, bytes_accessed=6 << 20, transcendentals=CH * TAPS),
    )(x, halo, taps, filt, rate[:, None], gain[None, :], jnp.asarray(forward), jnp.asarray(inverse))


def project_kernel(where_ref, acts_ref, *refs):
    n_src = len(PIECES)
    src, (out_ref, acts, weight, act_sems, w_sems) = refs[:n_src], refs[n_src:]
    y, z = where_ref[0], where_ref[1]
    for k in range(8):
        pltpu.make_async_copy(acts_ref.at[k], acts.at[k], act_sems.at[k]).start()
    pending = [[] for _ in range(4)]
    n = 0
    for ref, (kind, j_list, i_list) in zip(src, PIECES, strict=True):
        for a, j in enumerate(j_list):
            for e, i in enumerate(i_list):
                view = ref.at[e] if kind == "A" else ref.at[a]
                row = 0 if kind == "A" else CH // 2
                target = weight.at[i // 2, j, pl.ds(row, CH // 2), pl.ds((i % 2) * 128, 128)]
                pending[i // 2].append((n, view, target))
                n += 1
    copies = []
    for p in range(4):
        group = [pltpu.make_async_copy(view, target, w_sems.at[n]) for n, view, target in pending[p]]
        for copy in group:
            copy.start()
        copies.append(group)
    for k in range(8):
        pltpu.make_async_copy(acts_ref.at[k], acts.at[k], act_sems.at[k]).wait()
    for p in range(4):
        for copy in copies[p]:
            copy.wait()

        def rows_step(m, carry):
            start = pl.multiple_of((m % 2) * 256, 256)
            total = None
            for j in range(4):
                block = (m // 2) * 4 + lax.rem(y + j, 4)
                term = jnp.dot(acts[block, pl.ds(start, 256), :], weight[p, j], preferred_element_type=F32)
                total = term if total is None else total + term
            rounded = total.astype(BF16)
            row = pl.multiple_of(m * 256, 256)
            for e in range(2):
                col = pl.multiple_of(lax.rem(z + 2 * p + e, 8) * 128, 128)
                out_ref[pl.ds(row, 256), pl.ds(col, 128)] = rounded[:, e * 128 : (e + 1) * 128]
            return carry

        lax.fori_loop(0, 4, rows_step, 0)


PIECES = (
    [("A", [0], list(range(8))), ("A", [1], list(range(8))), ("A", [3], list(range(8)))]
    + [("A", [2], [0, 1, 2, 3]), ("A", [2], [4, 5, 6, 7])]
    + [("B", [0, 1, 2, 3], [i]) for i in (0, 1, 2, 3, 5, 6, 7)]
    + [("B", [0, 1], [4]), ("B", [2, 3], [4])]
)


def project(where, acts, pieces):
    any_space = pl.BlockSpec(memory_space=pl.ANY)
    n_copies = sum(len(j) * len(i) for _, j, i in PIECES)
    return pl.pallas_call(
        project_kernel,
        in_specs=[pl.BlockSpec(memory_space=pltpu.SMEM)] + [any_space] * (1 + len(pieces)),
        out_specs=pl.BlockSpec(memory_space=pltpu.VMEM),
        out_shape=jax.ShapeDtypeStruct((2 * TOK, CH), BF16),
        scratch_shapes=[
            pltpu.VMEM((8, TOK, CH), BF16),
            pltpu.VMEM((4, 4, CH, 256), BF16),
            pltpu.SemaphoreType.DMA((8,)),
            pltpu.SemaphoreType.DMA((n_copies,)),
        ],
        compiler_params=pltpu.CompilerParams(vmem_limit_bytes=48 << 20),
        cost_estimate=pl.CostEstimate(flops=2 * 1024 * 4096 * 1024, bytes_accessed=20 << 20, transcendentals=0),
    )(where, acts, *pieces)


def shift(value, axis, steps):
    size = lax.axis_size(axis)
    return lax.ppermute(value, axis, [(i, (i + steps) % size) for i in range(size)])


def gather_weight(own):
    a0, b0 = own[: CH // 2], own[CH // 2 :]
    a = {0: a0}
    for d in (1, 2, 3):
        a[d] = shift(a[d - 1], "z", -1)
        a[8 - d] = shift(a[(9 - d) % 8], "z", 1)
    a[4] = jnp.concatenate([shift(a[3][: CH // 4], "z", -1), shift(a[5][CH // 4 :], "z", 1)])
    b = {0: b0, 1: shift(b0, "y", -1), 3: shift(b0, "y", 1)}
    b[2] = jnp.concatenate([shift(b[1][: CH // 4], "y", -1), shift(b[3][CH // 4 :], "y", 1)])
    big_a = jnp.stack([a[i] for i in range(8)])
    big_b = jnp.stack([b[j] for j in range(4)])
    a1, a3 = shift(big_a, "y", -1), shift(big_a, "y", 1)
    a2_low, a2_high = shift(a1[:4], "y", -1), shift(a3[4:], "y", 1)
    up, down = {0: big_b}, {0: big_b}
    for d in (1, 2, 3):
        up[d] = shift(up[d - 1], "z", -1)
        down[d] = shift(down[d - 1], "z", 1)
    b4_low, b4_high = shift(up[3][:2], "z", -1), shift(down[3][2:], "z", 1)
    return [big_a, a1, a3, a2_low, a2_high, big_b, up[1], up[2], up[3], down[3], down[2], down[1], b4_low, b4_high]


def on_device(projected, short_taps, filter_taps, decay_rates, bypass_gain, out_weight):
    swap = [(y * 4 + t, t * 4 + y) for y in range(4) for t in range(4)]
    own = lax.ppermute(out_weight, ("y", "xl", "c"), swap)
    x = jnp.transpose(projected, (1, 0, 2))
    tail = tail_rows(x, short_taps)
    halo = lax.ppermute(tail, ("y", "xh", "z"), [(i, i + 1) for i in range(63)])
    gated = mixer(x, halo, short_taps, filter_taps, decay_rates, bypass_gain)
    acts = lax.all_gather(gated, CELL, axis=0, tiled=False)
    pieces = gather_weight(own)
    where = jnp.stack([lax.axis_index("y"), lax.axis_index("z")]).astype(jnp.int32)
    mine = project(where, acts, pieces)
    got = lax.all_to_all(mine.reshape(8, TOK // 4, CH), CELL, 0, 0, tiled=True)
    got = got.reshape(2, 4, TOK // 4, CH)
    return jnp.transpose(got, (2, 1, 0, 3)).reshape(TOK // 4, 8 * CH)


def solution(mesh):
    fine = Mesh(mesh.devices.reshape(4, 2, 8, 2, 2), ("y", "xh", "z", "xl", "c"))
    ctx, tp = ("y", "xh", "z"), ("xl", "c")
    return jax.shard_map(
        on_device,
        mesh=fine,
        in_specs=(P(ctx, None, tp), P(None, None, tp), P(tp, None), P(tp), P(tp), P(tp, ctx)),
        out_specs=P(ctx + tp, None),
        check_vma=False,
    )
```

time: 381 us -> 190 us (0.50)
  waiting for transfers between devices: 297 us -> 43.7 us
  matrix products: 46.2 us -> 0 us
  starting transfers between devices: 5.33 us -> 50.8 us
  blocking collectives: 0 us -> 37.4 us
  Pallas kernels: 0 us -> 24.9 us
  local copies, waits for them, and re-layouts: 8.4 us -> 18.1 us
  other arithmetic: 9.56 us -> 0.17 us
    all_gather x1, waiting for transfers between devices: 207 us -> 0.02 us  [on_device(): acts = lax.all_gather(gated, CELL, axis=0, tiled=False)]
    reduce_scatter x1 -> x0, waiting for transfers between devices: 80.9 us -> none  [on_device(): lax.psum_scatter(partial_value.astype(jnp.bfloat16), 'tp', scatter_dimens...]
    ppermute x1 -> x26, starting transfers between devices: 5.29 us -> 50.7 us  [the longest x24 33.7 us: shift(): lax.ppermute(value, axis, [(i, (i + steps) % size) for i in range(size)])]
    all_to_all x0 -> x1, blocking collectives: none -> 37.4 us  [on_device(): got = lax.all_to_all(mine.reshape(8, TOK // 4, CH), CELL, 0, 0, tiled=True)]
    ppermute x1 -> x26, waiting for transfers between devices: 9.31 us -> 43.7 us  [the longest x24 34.6 us: shift(): lax.ppermute(value, axis, [(i, (i + steps) % size) for i in range(size)])]
    conv_general_dilated x1 -> x0, matrix products: 31 us -> none  [causal_filter(): lax.conv_general_dilated(extended_products[None], kernel, (1,), 'VALID',...]
    pallas_call x0 -> x3, Pallas kernels: none -> 24.9 us  [the longest x1 17.9 us: project(): pl.pallas_call(project_kernel, in_specs=[pl.BlockSpec(memory_space=pltpu....]
    dot_general x1 -> x0, matrix products: 15.2 us -> none  [on_device(): jnp.dot(gated, lax.all_gather(out_weight, 'ctx', axis=1, tiled=True), pre...]
  transfers between devices with their start and end apart: 3 -> 27, of which waited for: 3 -> 10; matrix products, arithmetic and copies ran while one was open for 13% -> 2% of each run, Pallas kernels for 0% -> 0%
where the time goes in v1:
time: 190 us; the launch traced here: 189 us
  starting transfers between devices  50.8 us (27%)
  waiting for transfers between devices  43.7 us (23%)
  blocking collectives  37.4 us (20%)
  Pallas kernels  24.9 us (13%)
  local copies, waits for them, and re-layouts  18.1 us (10%)
  between operations  13.6 us (7%)
    all_to_all x1, blocking collectives, on_device(): got = lax.all_to_all(mine.reshape(8, TOK // 4, CH), CELL, 0, 0, tiled=True)  37.4 us
    ppermute x24, waiting for transfers between devices, shift(): lax.ppermute(value, axis, [(i, (i + steps) % size) for i in range(size)])  34.6 us
    ppermute x24, starting transfers between devices, shift(): lax.ppermute(value, axis, [(i, (i + steps) % size) for i in range(size)])  33.7 us
    pallas_call x1, Pallas kernels, project(): pl.pallas_call(project_kernel, in_specs=[pl.BlockSpec(memory_space=pltpu....  17.9 us
    ppermute x1, starting transfers between devices, on_device(): own = lax.ppermute(out_weight, ('y', 'xl', 'c'), swap)  11.8 us
    unnamed x40, local copies, waits for them, and re-layouts  8.78 us
    pallas_call x1, Pallas kernels, mixer(): pl.pallas_call(mixer_kernel, grid=(steps,), in_specs=[pl.BlockSpec((3, TO...  6.24 us
    ppermute x1, starting transfers between devices, on_device(): halo = lax.ppermute(tail, ('y', 'xh', 'z'), [(i, i + 1) for i in range(63)])  5.23 us
  transfers between devices with their start and end apart: 27, of which 10 were waited for; matrix products, arithmetic and copies ran while one was open for 2% of the time, Pallas kernels for 0%

profile of v1, /device:TPU:1, one launch (start us, length us, event | category | flops | bytes accessed | tf_op | source)
XLA Modules:
  0.0 188.7 jit_solution(8614397723368743747)
XLA Ops:
  10.0 5.2 %collective-permute-start = (bf16[144,1024]{1,0:T(8,128)(2,1)S(1)}, bf16[144,1024]{1,0:T(8,128)(2,1)}, u32[]{:S(2)}, u32[]{:S(2)}) collective-permute-start(bf16[144,1024]{1,0:T(8,128)(2,1)S(1)} %shard_map.82), channel_id=1, source_target_pairs={{0,4},{4,8},{8,12},{12,16},{16,20},{20,24},{24,28},{28,32},{32,36}... | collective-permute-start | bytes 884744 | tf_op jit(solution)/shard_map/ppermute | solution.py:257
  16.2 3.9 %collective-permute-done.halo_ref = bf16[144,1024]{1,0:T(8,128)(2,1)} collective-permute-done((bf16[144,1024]{1,0:T(8,128)(2,1)S(1)}, bf16[144,1024]{1,0:T(8,128)(2,1)}, u32[]{:S(2)}, u32[]{:S(2)}) %collective-permute-start) | collective-permute-done | bytes 294944 | tf_op jit(solution)/shard_map/ppermute | solution.py:257
  24.1 6.2 %shard_map.83 = bf16[512,1024]{1,0:T(8,128)(2,1)S(1)} custom-call(bf16[3,512,1024]{2,1,0:T(8,128)(2,1)S(1)} %bitcast.36, bf16[144,1024]{1,0:T(8,128)(2,1)} %collective-permute-done.halo_ref, f32[3,3,1024]{2,1,0:T(4,128)S(1)} %copy-done.5, f32[1024,128]{1,0:T(8,128)S(1)} %copy-done.6, f32[1024,1]{1,0:T(8,128)S(1)} %copy-done.3, f32[1,1024]{1,0:T(1,128)S(1)} %bitcast.37, ...), custom_call_target="tpu_custom_call" | custom-call | flops 1800000000 | bytes 6291456 | tf_op jit(solution)/shard_map/pallas_call | solution.py:130
  31.4 11.8 %collective-permute-start.1 = (bf16[1024,128]{1,0:T(8,128)(2,1)S(1)}, bf16[1024,128]{1,0:T(8,128)(2,1)S(1)}, u32[]{:S(2)}, u32[]{:S(2)}) collective-permute-start(bf16[1024,128]{1,0:T(8,128)(2,1)S(1)} %copy-done.16), channel_id=1, source_target_pairs={{0,0},{1,64},{2,128},{3,192},{64,1},{65,65},{66,129},{67,193},{128... | collective-permute-start | bytes 786440 | tf_op jit(solution)/shard_map/ppermute | solution.py:254
  43.2 5.1 %collective-permute-done.1 = bf16[1024,128]{1,0:T(8,128)(2,1)S(1)} collective-permute-done((bf16[1024,128]{1,0:T(8,128)(2,1)S(1)}, bf16[1024,128]{1,0:T(8,128)(2,1)S(1)}, u32[]{:S(2)}, u32[]{:S(2)}) %collective-permute-start.1) | collective-permute-done | bytes 262176 | tf_op jit(solution)/shard_map/ppermute | solution.py:254
  48.4 5.9 %collective-permute-start.14 = (bf16[512,128]{1,0:T(8,128)(2,1)S(1)}, bf16[512,128]{1,0:T(8,128)(2,1)S(1)}, u32[]{:S(2)}, u32[]{:S(2)}) collective-permute-start(bf16[512,128]{1,0:T(8,128)(2,1)S(1)} %get-tuple-element.6), channel_id=1, source_target_pairs={{0,192},{64,0},{128,64},{192,128},{1,193},{65,1},{129,65},{193,129... | collective-permute-start | bytes 393224 | tf_op jit(solution)/shard_map/ppermute | solution.py:228
  56.2 3.5 %collective-permute-start.15 = (bf16[256,128]{1,0:T(8,128)(2,1)S(1)}, bf16[256,128]{1,0:T(8,128)(2,1)S(1)}, u32[]{:S(2)}, u32[]{:S(2)}) collective-permute-start(bf16[256,128]{1,0:T(8,128)(2,1)S(1)} %slice.46), channel_id=1, source_target_pairs={{0,192},{64,0},{128,64},{192,128},{1,193},{65,1},{129,65},{193,129... | collective-permute-start | bytes 196616 | tf_op jit(solution)/shard_map/ppermute | solution.py:228
  61.4 3.1 %collective-permute-done.17 = bf16[256,128]{1,0:T(8,128)(2,1)S(1)} collective-permute-done((bf16[256,128]{1,0:T(8,128)(2,1)S(1)}, bf16[256,128]{1,0:T(8,128)(2,1)S(1)}, u32[]{:S(2)}, u32[]{:S(2)}) %collective-permute-start.17) | collective-permute-done | bytes 65568 | tf_op jit(solution)/shard_map/ppermute | solution.py:228
  64.7 2.7 %collective-permute-start.18 = (bf16[4,512,128]{2,1,0:T(8,128)(2,1)S(1)}, bf16[4,512,128]{2,1,0:T(8,128)(2,1)S(1)}, u32[]{:S(2)}, u32[]{:S(2)}) collective-permute-start(bf16[4,512,128]{2,1,0:T(8,128)(2,1)S(1)} %pad_maximum_fusion.refs_5_), channel_id=1, source_target_pairs={{0,28},{4,0},{8,4},{12,8},{16,12},{20,16},{24,20},{28,24},{1,29},{... | collective-permute-start | bytes 1572872 | tf_op jit(solution)/shard_map/ppermute | solution.py:228
  68.9 9.3 %collective-permute-done.4 = bf16[512,128]{1,0:T(8,128)(2,1)S(1)} collective-permute-done((bf16[512,128]{1,0:T(8,128)(2,1)S(1)}, bf16[512,128]{1,0:T(8,128)(2,1)S(1)}, u32[]{:S(2)}, u32[]{:S(2)}) %collective-permute-start.4) | collective-permute-done | bytes 131104 | tf_op jit(solution)/shard_map/ppermute | solution.py:228
  78.2 3.5 %collective-permute-start.5 = (bf16[256,128]{1,0:T(8,128)(2,1)S(1)}, bf16[256,128]{1,0:T(8,128)(2,1)S(1)}, u32[]{:S(2)}, u32[]{:S(2)}) collective-permute-start(bf16[256,128]{1,0:T(8,128)(2,1)S(1)} %slice.41), channel_id=1, source_target_pairs={{0,28},{4,0},{8,4},{12,8},{16,12},{20,16},{24,20},{28,24},{1,29},{... | collective-permute-start | bytes 196616 | tf_op jit(solution)/shard_map/ppermute | solution.py:228
  83.0 3.5 %collective-permute-done.9 = bf16[256,128]{1,0:T(8,128)(2,1)S(1)} collective-permute-done((bf16[256,128]{1,0:T(8,128)(2,1)S(1)}, bf16[256,128]{1,0:T(8,128)(2,1)S(1)}, u32[]{:S(2)}, u32[]{:S(2)}) %collective-permute-start.9) | collective-permute-done | bytes 65568 | tf_op jit(solution)/shard_map/ppermute | solution.py:228
  86.7 2.7 %collective-permute-start.10 = (bf16[8,512,128]{2,1,0:T(8,128)(2,1)S(1)}, bf16[8,512,128]{2,1,0:T(8,128)(2,1)S(1)}, u32[]{:S(2)}, u32[]{:S(2)}) collective-permute-start(bf16[8,512,128]{2,1,0:T(8,128)(2,1)S(1)} %bitcast_dynamic-update-slice_fusion.refs_0_), channel_id=1, source_target_pairs={{0,192},{64,0},{128,64},{192,128},{1,193},{65,1},{129,65},{193,129... | collective-permute-start | bytes 3145736 | tf_op jit(solution)/shard_map/ppermute | solution.py:228
  89.4 2.7 %collective-permute-start.19 = (bf16[4,512,128]{2,1,0:T(8,128)(2,1)S(1)}, bf16[4,512,128]{2,1,0:T(8,128)(2,1)S(1)}, u32[]{:S(2)}, u32[]{:S(2)}) collective-permute-start(bf16[4,512,128]{2,1,0:T(8,128)(2,1)S(1)} %collective-permute-done.18.refs_6_), channel_id=1, source_target_pairs={{0,28},{4,0},{8,4},{12,8},{16,12},{20,16},{24,20},{28,24},{1,29},{... | collective-permute-start | bytes 1572872 | tf_op jit(solution)/shard_map/ppermute | solution.py:228
  92.0 6.9 %collective-permute-done.22.refs_10_ = bf16[4,512,128]{2,1,0:T(8,128)(2,1)S(1)} collective-permute-done((bf16[4,512,128]{2,1,0:T(8,128)(2,1)S(1)}, bf16[4,512,128]{2,1,0:T(8,128)(2,1)S(1)}, u32[]{:S(2)}, u32[]{:S(2)}) %collective-permute-start.22) | collective-permute-done | bytes 524320 | tf_op jit(solution)/shard_map/ppermute | solution.py:228
  98.9 2.7 %collective-permute-start.20 = (bf16[4,512,128]{2,1,0:T(8,128)(2,1)S(1)}, bf16[4,512,128]{2,1,0:T(8,128)(2,1)S(1)}, u32[]{:S(2)}, u32[]{:S(2)}) collective-permute-start(bf16[4,512,128]{2,1,0:T(8,128)(2,1)S(1)} %collective-permute-done.19.refs_7_), channel_id=1, source_target_pairs={{0,28},{4,0},{8,4},{12,8},{16,12},{20,16},{24,20},{28,24},{1,29},{... | collective-permute-start | bytes 1572872 | tf_op jit(solution)/shard_map/ppermute | solution.py:228
  101.6 5.9 %collective-permute-done.11.refs_2_ = bf16[8,512,128]{2,1,0:T(8,128)(2,1)S(1)} collective-permute-done((bf16[8,512,128]{2,1,0:T(8,128)(2,1)S(1)}, bf16[8,512,128]{2,1,0:T(8,128)(2,1)S(1)}, u32[]{:S(2)}, u32[]{:S(2)}) %collective-permute-start.11) | collective-permute-done | bytes 1048608 | tf_op jit(solution)/shard_map/ppermute | solution.py:228
  109.2 2.7 %collective-permute-start.12 = (bf16[4,512,128]{2,1,0:T(8,128)(2,1)}, bf16[4,512,128]{2,1,0:T(8,128)(2,1)}, u32[]{:S(2)}, u32[]{:S(2)}) collective-permute-start(bf16[4,512,128]{2,1,0:T(8,128)(2,1)} %slice.43), channel_id=1, source_target_pairs={{0,192},{64,0},{128,64},{192,128},{1,193},{65,1},{129,65},{193,129... | collective-permute-start | bytes 1572872 | tf_op jit(solution)/shard_map/ppermute | solution.py:228
  113.4 2.7 %collective-permute-start.24 = (bf16[2,512,128]{2,1,0:T(8,128)(2,1)}, bf16[2,512,128]{2,1,0:T(8,128)(2,1)}, u32[]{:S(2)}, u32[]{:S(2)}) collective-permute-start(bf16[2,512,128]{2,1,0:T(8,128)(2,1)} %slice.48), channel_id=1, source_target_pairs={{0,28},{4,0},{8,4},{12,8},{16,12},{20,16},{24,20},{28,24},{1,29},{... | collective-permute-start | bytes 786440 | tf_op jit(solution)/shard_map/ppermute | solution.py:228
  116.1 4.3 %collective-permute-done.25.refs_13_ = bf16[2,512,128]{2,1,0:T(8,128)(2,1)S(1)} collective-permute-done((bf16[2,512,128]{2,1,0:T(8,128)(2,1)}, bf16[2,512,128]{2,1,0:T(8,128)(2,1)S(1)}, u32[]{:S(2)}, u32[]{:S(2)}) %collective-permute-start.25) | collective-permute-done | bytes 262176 | tf_op jit(solution)/shard_map/ppermute | solution.py:228
  121.5 17.9 %shard_map.84 = bf16[1024,1024]{1,0:T(8,128)(2,1)} custom-call(s32[2]{0:T(128)S(1)} %pad_add_fusion.where_ref, bf16[8,512,1024]{2,1,0:T(8,128)(2,1)} %bitcast.44, bf16[8,512,128]{2,1,0:T(8,128)(2,1)} %copy-done.14, bf16[8,512,128]{2,1,0:T(8,128)(2,1)} %copy-done.13, bf16[8,512,128]{2,1,0:T(8,128)(2,1)} %copy-done.12, ...), custom_call_target="tpu_custom_call" | custom-call | flops 8589934592 | bytes 20971520 | tf_op jit(solution)/shard_map/pallas_call | solution.py:210
  139.5 37.4 %all_to_all.5 = bf16[8,128,1024]{2,1,0:T(8,128)(2,1)S(1)} all-to-all(bf16[8,128,1024]{2,1,0:T(8,128)(2,1)} %bitcast.40), channel_id=1, replica_groups=mesh['y'=4,'xh'=2,'z'=8,'xl'=2,'c'=2] {'xh','xl','c'}, dimensions={0} | all-to-all | bytes 4194304 | tf_op jit(solution)/shard_map/all_to_all | solution.py:263
  176.9 2.2 %copy.13 = bf16[2,4,128,1024]{3,0,1,2:T(2,128)(2,1)S(1)} copy(bf16[2,4,128,1024]{3,2,1,0:T(8,128)(2,1)S(1)} %bitcast.38) | data formatting | bytes 4194304 | tf_op jit(solution)/shard_map/reshape | solution.py:264
  179.1 2.8 %reshape.11 = bf16[128,8192]{1,0:T(8,128)(2,1)} reshape(bf16[128,4,2,1024]{3,2,1,0:T(2,128)(2,1)S(1)} %bitcast.39) | data formatting | bytes 4194304 | tf_op jit(solution)/shard_map/reshape | solution.py:265
  (92 shorter events, 20.6 us)
Async XLA Ops:
  6.5 113.9 %all-gather.3.cloned.1.call-start = ((), (), s32[]{:S(2)}) async-start(), calls=%async_computation.1 | async-start | bytes 9437184 | tf_op jit(solution)/shard_map/all_gather | solution.py:259
  10.0 10.2 %collective-permute-start = (bf16[144,1024]{1,0:T(8,128)(2,1)S(1)}, bf16[144,1024]{1,0:T(8,128)(2,1)}, u32[]{:S(2)}, u32[]{:S(2)}) collective-permute-start(bf16[144,1024]{1,0:T(8,128)(2,1)S(1)} %shard_map.82), channel_id=1, source_target_pairs={{0,4},{4,8},{8,12},{12,16},{16,20},{20,24},{24,28},{28,32},{32,36}... | collective-permute-start | bytes 884744 | tf_op jit(solution)/shard_map/ppermute | solution.py:257
  31.4 16.9 %collective-permute-start.1 = (bf16[1024,128]{1,0:T(8,128)(2,1)S(1)}, bf16[1024,128]{1,0:T(8,128)(2,1)S(1)}, u32[]{:S(2)}, u32[]{:S(2)}) collective-permute-start(bf16[1024,128]{1,0:T(8,128)(2,1)S(1)} %copy-done.16), channel_id=1, source_target_pairs={{0,0},{1,64},{2,128},{3,192},{64,1},{65,65},{66,129},{67,193},{128... | collective-permute-start | bytes 786440 | tf_op jit(solution)/shard_map/ppermute | solution.py:254
  48.4 7.9 %collective-permute-start.14 = (bf16[512,128]{1,0:T(8,128)(2,1)S(1)}, bf16[512,128]{1,0:T(8,128)(2,1)S(1)}, u32[]{:S(2)}, u32[]{:S(2)}) collective-permute-start(bf16[512,128]{1,0:T(8,128)(2,1)S(1)} %get-tuple-element.6), channel_id=1, source_target_pairs={{0,192},{64,0},{128,64},{192,128},{1,193},{65,1},{129,65},{193,129... | collective-permute-start | bytes 393224 | tf_op jit(solution)/shard_map/ppermute | solution.py:228
  54.3 5.4 %collective-permute-start.16 = (bf16[512,128]{1,0:T(8,128)(2,1)S(1)}, bf16[512,128]{1,0:T(8,128)(2,1)S(1)}, u32[]{:S(2)}, u32[]{:S(2)}) collective-permute-start(bf16[512,128]{1,0:T(8,128)(2,1)S(1)} %get-tuple-element.6), channel_id=1, source_target_pairs={{0,64},{64,128},{128,192},{192,0},{1,65},{65,129},{129,193},{193,1... | collective-permute-start | bytes 393224 | tf_op jit(solution)/shard_map/ppermute | solution.py:228
  54.3 5.5 %collective-permute-start.2 = (bf16[512,128]{1,0:T(8,128)(2,1)S(1)}, bf16[512,128]{1,0:T(8,128)(2,1)S(1)}, u32[]{:S(2)}, u32[]{:S(2)}) collective-permute-start(bf16[512,128]{1,0:T(8,128)(2,1)S(1)} %get-tuple-element.7), channel_id=1, source_target_pairs={{0,28},{4,0},{8,4},{12,8},{16,12},{20,16},{24,20},{28,24},{1,29},{... | collective-permute-start | bytes 393224 | tf_op jit(solution)/shard_map/ppermute | solution.py:228
  54.3 5.7 %collective-permute-start.6 = (bf16[512,128]{1,0:T(8,128)(2,1)S(1)}, bf16[512,128]{1,0:T(8,128)(2,1)S(1)}, u32[]{:S(2)}, u32[]{:S(2)}) collective-permute-start(bf16[512,128]{1,0:T(8,128)(2,1)S(1)} %get-tuple-element.7), channel_id=1, source_target_pairs={{0,4},{4,8},{8,12},{12,16},{16,20},{20,24},{24,28},{28,0},{1,5},{5... | collective-permute-start | bytes 393224 | tf_op jit(solution)/shard_map/ppermute | solution.py:228
  56.2 5.2 %collective-permute-start.15 = (bf16[256,128]{1,0:T(8,128)(2,1)S(1)}, bf16[256,128]{1,0:T(8,128)(2,1)S(1)}, u32[]{:S(2)}, u32[]{:S(2)}) collective-permute-start(bf16[256,128]{1,0:T(8,128)(2,1)S(1)} %slice.46), channel_id=1, source_target_pairs={{0,192},{64,0},{128,64},{192,128},{1,193},{65,1},{129,65},{193,129... | collective-permute-start | bytes 196616 | tf_op jit(solution)/shard_map/ppermute | solution.py:228
  59.8 7.6 %collective-permute-start.3 = (bf16[512,128]{1,0:T(8,128)(2,1)S(1)}, bf16[512,128]{1,0:T(8,128)(2,1)S(1)}, u32[]{:S(2)}, u32[]{:S(2)}) collective-permute-start(bf16[512,128]{1,0:T(8,128)(2,1)S(1)} %collective-permute-done.2), channel_id=1, source_target_pairs={{0,28},{4,0},{8,4},{12,8},{16,12},{20,16},{24,20},{28,24},{1,29},{... | collective-permute-start | bytes 393224 | tf_op jit(solution)/shard_map/ppermute | solution.py:228
  59.9 7.5 %collective-permute-start.7 = (bf16[512,128]{1,0:T(8,128)(2,1)S(1)}, bf16[512,128]{1,0:T(8,128)(2,1)S(1)}, u32[]{:S(2)}, u32[]{:S(2)}) collective-permute-start(bf16[512,128]{1,0:T(8,128)(2,1)S(1)} %collective-permute-done.6), channel_id=1, source_target_pairs={{0,4},{4,8},{8,12},{12,16},{16,20},{20,24},{24,28},{28,0},{1,5},{5... | collective-permute-start | bytes 393224 | tf_op jit(solution)/shard_map/ppermute | solution.py:228
  64.6 24.7 %collective-permute-start.21 = (bf16[4,512,128]{2,1,0:T(8,128)(2,1)S(1)}, bf16[4,512,128]{2,1,0:T(8,128)(2,1)S(1)}, u32[]{:S(2)}, u32[]{:S(2)}) collective-permute-start(bf16[4,512,128]{2,1,0:T(8,128)(2,1)S(1)} %pad_maximum_fusion.refs_5_), channel_id=1, source_target_pairs={{0,4},{4,8},{8,12},{12,16},{16,20},{20,24},{24,28},{28,0},{1,5},{5... | collective-permute-start | bytes 1572872 | tf_op jit(solution)/shard_map/ppermute | solution.py:228
  64.7 24.7 %collective-permute-start.18 = (bf16[4,512,128]{2,1,0:T(8,128)(2,1)S(1)}, bf16[4,512,128]{2,1,0:T(8,128)(2,1)S(1)}, u32[]{:S(2)}, u32[]{:S(2)}) collective-permute-start(bf16[4,512,128]{2,1,0:T(8,128)(2,1)S(1)} %pad_maximum_fusion.refs_5_), channel_id=1, source_target_pairs={{0,28},{4,0},{8,4},{12,8},{16,12},{20,16},{24,20},{28,24},{1,29},{... | collective-permute-start | bytes 1572872 | tf_op jit(solution)/shard_map/ppermute | solution.py:228
  67.4 10.8 %collective-permute-start.4 = (bf16[512,128]{1,0:T(8,128)(2,1)S(1)}, bf16[512,128]{1,0:T(8,128)(2,1)S(1)}, u32[]{:S(2)}, u32[]{:S(2)}) collective-permute-start(bf16[512,128]{1,0:T(8,128)(2,1)S(1)} %collective-permute-done.3), channel_id=1, source_target_pairs={{0,28},{4,0},{8,4},{12,8},{16,12},{20,16},{24,20},{28,24},{1,29},{... | collective-permute-start | bytes 393224 | tf_op jit(solution)/shard_map/ppermute | solution.py:228
  67.4 14.3 %collective-permute-start.8 = (bf16[512,128]{1,0:T(8,128)(2,1)S(1)}, bf16[512,128]{1,0:T(8,128)(2,1)S(1)}, u32[]{:S(2)}, u32[]{:S(2)}) collective-permute-start(bf16[512,128]{1,0:T(8,128)(2,1)S(1)} %collective-permute-done.7), channel_id=1, source_target_pairs={{0,4},{4,8},{8,12},{12,16},{16,20},{20,24},{24,28},{28,0},{1,5},{5... | collective-permute-start | bytes 393224 | tf_op jit(solution)/shard_map/ppermute | solution.py:228
  86.6 20.8 %collective-permute-start.11 = (bf16[8,512,128]{2,1,0:T(8,128)(2,1)S(1)}, bf16[8,512,128]{2,1,0:T(8,128)(2,1)S(1)}, u32[]{:S(2)}, u32[]{:S(2)}) collective-permute-start(bf16[8,512,128]{2,1,0:T(8,128)(2,1)S(1)} %bitcast_dynamic-update-slice_fusion.refs_0_), channel_id=1, source_target_pairs={{0,64},{64,128},{128,192},{192,0},{1,65},{65,129},{129,193},{193,1... | collective-permute-start | bytes 3145736 | tf_op jit(solution)/shard_map/ppermute | solution.py:228
  86.7 21.7 %collective-permute-start.10 = (bf16[8,512,128]{2,1,0:T(8,128)(2,1)S(1)}, bf16[8,512,128]{2,1,0:T(8,128)(2,1)S(1)}, u32[]{:S(2)}, u32[]{:S(2)}) collective-permute-start(bf16[8,512,128]{2,1,0:T(8,128)(2,1)S(1)} %bitcast_dynamic-update-slice_fusion.refs_0_), channel_id=1, source_target_pairs={{0,192},{64,0},{128,64},{192,128},{1,193},{65,1},{129,65},{193,129... | collective-permute-start | bytes 3145736 | tf_op jit(solution)/shard_map/ppermute | solution.py:228
  89.4 9.5 %collective-permute-start.22 = (bf16[4,512,128]{2,1,0:T(8,128)(2,1)S(1)}, bf16[4,512,128]{2,1,0:T(8,128)(2,1)S(1)}, u32[]{:S(2)}, u32[]{:S(2)}) collective-permute-start(bf16[4,512,128]{2,1,0:T(8,128)(2,1)S(1)} %collective-permute-done.21.refs_11_), channel_id=1, source_target_pairs={{0,4},{4,8},{8,12},{12,16},{16,20},{20,24},{24,28},{28,0},{1,5},{5... | collective-permute-start | bytes 1572872 | tf_op jit(solution)/shard_map/ppermute | solution.py:228
  89.4 9.5 %collective-permute-start.19 = (bf16[4,512,128]{2,1,0:T(8,128)(2,1)S(1)}, bf16[4,512,128]{2,1,0:T(8,128)(2,1)S(1)}, u32[]{:S(2)}, u32[]{:S(2)}) collective-permute-start(bf16[4,512,128]{2,1,0:T(8,128)(2,1)S(1)} %collective-permute-done.18.refs_6_), channel_id=1, source_target_pairs={{0,28},{4,0},{8,4},{12,8},{16,12},{20,16},{24,20},{28,24},{1,29},{... | collective-permute-start | bytes 1572872 | tf_op jit(solution)/shard_map/ppermute | solution.py:228
  98.9 13.0 %collective-permute-start.23 = (bf16[4,512,128]{2,1,0:T(8,128)(2,1)S(1)}, bf16[4,512,128]{2,1,0:T(8,128)(2,1)S(1)}, u32[]{:S(2)}, u32[]{:S(2)}) collective-permute-start(bf16[4,512,128]{2,1,0:T(8,128)(2,1)S(1)} %collective-permute-done.22.refs_10_), channel_id=1, source_target_pairs={{0,4},{4,8},{8,12},{12,16},{16,20},{20,24},{24,28},{28,0},{1,5},{5... | collective-permute-start | bytes 1572872 | tf_op jit(solution)/shard_map/ppermute | solution.py:228
  98.9 13.7 %collective-permute-start.20 = (bf16[4,512,128]{2,1,0:T(8,128)(2,1)S(1)}, bf16[4,512,128]{2,1,0:T(8,128)(2,1)S(1)}, u32[]{:S(2)}, u32[]{:S(2)}) collective-permute-start(bf16[4,512,128]{2,1,0:T(8,128)(2,1)S(1)} %collective-permute-done.19.refs_7_), channel_id=1, source_target_pairs={{0,28},{4,0},{8,4},{12,8},{16,12},{20,16},{24,20},{28,24},{1,29},{... | collective-permute-start | bytes 1572872 | tf_op jit(solution)/shard_map/ppermute | solution.py:228
  108.3 12.1 %collective-permute-start.13 = (bf16[4,512,128]{2,1,0:T(8,128)(2,1)}, bf16[4,512,128]{2,1,0:T(8,128)(2,1)}, u32[]{:S(2)}, u32[]{:S(2)}) collective-permute-start(bf16[4,512,128]{2,1,0:T(8,128)(2,1)} %slice.44), channel_id=1, source_target_pairs={{0,64},{64,128},{128,192},{192,0},{1,65},{65,129},{129,193},{193,1... | collective-permute-start | bytes 1572872 | tf_op jit(solution)/shard_map/ppermute | solution.py:228
  109.2 11.2 %collective-permute-start.12 = (bf16[4,512,128]{2,1,0:T(8,128)(2,1)}, bf16[4,512,128]{2,1,0:T(8,128)(2,1)}, u32[]{:S(2)}, u32[]{:S(2)}) collective-permute-start(bf16[4,512,128]{2,1,0:T(8,128)(2,1)} %slice.43), channel_id=1, source_target_pairs={{0,192},{64,0},{128,64},{192,128},{1,193},{65,1},{129,65},{193,129... | collective-permute-start | bytes 1572872 | tf_op jit(solution)/shard_map/ppermute | solution.py:228
  112.6 7.8 %collective-permute-start.25 = (bf16[2,512,128]{2,1,0:T(8,128)(2,1)}, bf16[2,512,128]{2,1,0:T(8,128)(2,1)S(1)}, u32[]{:S(2)}, u32[]{:S(2)}) collective-permute-start(bf16[2,512,128]{2,1,0:T(8,128)(2,1)} %slice.49), channel_id=1, source_target_pairs={{0,4},{4,8},{8,12},{12,16},{16,20},{20,24},{24,28},{28,0},{1,5},{5... | collective-permute-start | bytes 786440 | tf_op jit(solution)/shard_map/ppermute | solution.py:228
  113.4 7.1 %collective-permute-start.24 = (bf16[2,512,128]{2,1,0:T(8,128)(2,1)}, bf16[2,512,128]{2,1,0:T(8,128)(2,1)}, u32[]{:S(2)}, u32[]{:S(2)}) collective-permute-start(bf16[2,512,128]{2,1,0:T(8,128)(2,1)} %slice.48), channel_id=1, source_target_pairs={{0,28},{4,0},{8,4},{12,8},{16,12},{20,16},{24,20},{28,24},{1,29},{... | collective-permute-start | bytes 786440 | tf_op jit(solution)/shard_map/ppermute | solution.py:228
  (20 other events, 126.0 us)
Sparse Core Ops, SparseCore 0:
  31.5 58.3 all-gather.2

commit v2 on v1

v2 whole, which is shorter than its diff:
```python
import functools

import jax
import jax.numpy as jnp
import ml_dtypes
import numpy as np
from jax import lax
from jax.experimental import pallas as pl
from jax.experimental.pallas import tpu as pltpu
from jax.sharding import Mesh
from jax.sharding import PartitionSpec as P

TOK = 512
CH = 1024
TAPS = 128
WIN = 256
LANES = 256
CHUNKS = ((0, 1, 7, 2, 6), (3, 5, 4))
VMEM = 56 << 20
F32, BF16 = jnp.float32, jnp.bfloat16


def two_halves(matrix):
    high = matrix.astype(ml_dtypes.bfloat16)
    low = (matrix - high.astype(np.float64)).astype(ml_dtypes.bfloat16)
    return high, low


@functools.lru_cache(maxsize=None)
def transform_matrices():
    at = np.arange(WIN)
    half = WIN // 2
    angle = 2 * np.pi * (np.outer(np.arange(half), at) % WIN) / WIN
    sine = -np.sin(angle)
    sine[0] = np.cos(np.pi * at)
    forward = np.concatenate([np.cos(angle), sine])
    scale = np.where(np.arange(half) == 0, 1.0, 2.0)[:, None] / WIN
    scale_im = np.where(np.arange(half) == 0, 1.0, 2.0)[:, None] / WIN
    inverse = np.concatenate([np.cos(angle) * scale, sine * scale_im]).T[half:]
    fh, fl = two_halves(forward)
    ih, il = two_halves(inverse)
    return np.concatenate([fh, fl]), np.concatenate([ih, ih, il], axis=1)


def rolled(x, steps):
    return pltpu.roll(x, steps % x.shape[0], 0)


def featurize(rows, taps, count):
    lead = rows.shape[0] - count
    one = rolled(rows, 1)[lead:]
    two = rolled(rows, 2)[lead:]
    return (taps[0] * rows[lead:] + taps[1] * one + taps[2] * two).astype(BF16)


def tail_kernel(x_ref, before_ref, taps_ref, out_ref):
    streams = []
    raw = []
    for s in range(3):
        rows = x_ref[s].astype(F32)
        raw.append(rows[-8:])
        if s:
            taps = [taps_ref[j, s : s + 1, :] for j in range(3)]
            rows = jnp.concatenate([before_ref[s].astype(F32), rows], axis=0)
            streams.append(featurize(rows, taps, TAPS).astype(F32))
    out_ref[:TAPS, :] = (streams[0] * streams[1]).astype(BF16)
    row = lax.broadcasted_iota(jnp.int32, raw[0].shape, 0)
    packed = jnp.where(row < 2, rolled(raw[0], 2), jnp.where(row < 4, rolled(raw[1], 4), rolled(raw[2], 6)))
    out_ref[TAPS:, :] = jnp.concatenate([packed, jnp.zeros_like(packed)], axis=0).astype(BF16)


def tail_rows(x, taps):
    width = CH // 2
    return pl.pallas_call(
        tail_kernel,
        grid=(CH // width,),
        in_specs=[
            pl.BlockSpec((3, TAPS, width), lambda i: (0, TOK // TAPS - 1, i)),
            pl.BlockSpec((3, 16, width), lambda i: (0, (TOK - TAPS) // 16 - 1, i)),
            pl.BlockSpec((3, 3, width), lambda i: (0, 0, i)),
        ],
        out_specs=pl.BlockSpec((TAPS + 16, width), lambda i: (0, i)),
        out_shape=jax.ShapeDtypeStruct((TAPS + 16, CH), BF16),
        compiler_params=pltpu.CompilerParams(vmem_limit_bytes=VMEM),
        cost_estimate=pl.CostEstimate(flops=4 * TAPS * CH, bytes_accessed=2 << 20, transcendentals=0),
    )(x, x, taps)


def mixer_kernel(x_ref, halo_ref, taps_ref, filt_ref, rate_ref, gain_ref, fwd_ref, inv_ref, out_ref, prod, query):
    dot = functools.partial(lax.dot_general, preferred_element_type=F32)
    plain = (((1,), (0,)), ((), ()))
    half = WIN // 2

    lag = lax.broadcasted_iota(jnp.int32, (TAPS, LANES), 0).astype(F32)
    bank = (filt_ref[...].T * jnp.exp(-rate_ref[...] * lag)).astype(BF16)
    both = dot(fwd_ref[:, :half], bank, plain)
    spectrum = both[:WIN] + both[WIN:]
    h_re, h_im = spectrum[:half], spectrum[half:]
    first = lax.broadcasted_iota(jnp.int32, h_re.shape, 0) == 0
    h_last = jnp.where(first, h_im, h_re)
    h_im = jnp.where(first, 0.0, h_im)

    prod[:TAPS] = halo_ref[:TAPS]
    raw = halo_ref[TAPS:].astype(F32)[:8]
    for b in range(TOK // TAPS):
        made = []
        for s in range(3):
            taps = [taps_ref[j, s : s + 1, :] for j in range(3)]
            if b:
                rows = x_ref[s, b * TAPS - 16 : (b + 1) * TAPS, :].astype(F32)
            else:
                rows = jnp.concatenate([rolled(raw, 6 - 2 * s), x_ref[s, :TAPS, :].astype(F32)], axis=0)
            made.append(featurize(rows, taps, TAPS))
        query[b * TAPS : (b + 1) * TAPS] = made[0]
        prod[(b + 1) * TAPS : (b + 2) * TAPS] = (made[1].astype(F32) * made[2].astype(F32)).astype(BF16)

    for b in range(TOK // TAPS):
        both = dot(fwd_ref[...], prod[b * TAPS : b * TAPS + WIN], plain)
        spectrum = both[:WIN] + both[WIN:]
        re, im = spectrum[:half], spectrum[half:]
        y = jnp.concatenate([re * h_re - im * h_im, re * h_im + im * h_last], axis=0)
        high = y.astype(BF16)
        low = (y - high.astype(F32)).astype(BF16)
        long_part = dot(inv_ref[...], jnp.concatenate([high, low, high], axis=0), plain)
        here = prod[(b + 1) * TAPS : (b + 2) * TAPS].astype(F32)
        q = query[b * TAPS : (b + 1) * TAPS].astype(F32)
        out_ref[b * TAPS : (b + 1) * TAPS, :] = (q * (long_part + gain_ref[...] * here)).astype(BF16)


def mixer(x, halo, taps, filt, rate, gain):
    forward, inverse = transform_matrices()
    steps = CH // LANES
    return pl.pallas_call(
        mixer_kernel,
        grid=(steps,),
        in_specs=[
            pl.BlockSpec((3, TOK, LANES), lambda i: (0, 0, i)),
            pl.BlockSpec((TAPS + 16, LANES), lambda i: (0, i)),
            pl.BlockSpec((3, 3, LANES), lambda i: (0, 0, i)),
            pl.BlockSpec((LANES, TAPS), lambda i: (i, 0)),
            pl.BlockSpec((1, LANES), lambda i: (0, i)),
            pl.BlockSpec((1, LANES), lambda i: (0, i)),
            pl.BlockSpec(forward.shape, lambda i: (0, 0)),
            pl.BlockSpec(inverse.shape, lambda i: (0, 0)),
        ],
        out_specs=pl.BlockSpec((TOK, LANES), lambda i: (0, i)),
        out_shape=jax.ShapeDtypeStruct((TOK, CH), BF16),
        scratch_shapes=[
            pltpu.VMEM((TOK + TAPS, LANES), BF16),
            pltpu.VMEM((TOK, LANES), BF16),
        ],
        compiler_params=pltpu.CompilerParams(vmem_limit_bytes=VMEM),
        cost_estimate=pl.CostEstimate(flops=2 * 900 * 10**6, bytes_accessed=6 << 20, transcendentals=CH * TAPS),
    )(x, halo, taps, filt, rate[None, :], gain[None, :], jnp.asarray(forward), jnp.asarray(inverse))


def k_block(y, kind):
    if kind > 1:
        y = lax.rem(y + (1 if kind == 2 else 3), 4)
    return lax.rem(y, 2) * 2 + (1 - y // 2 if kind == 1 else y // 2)


def project_kernel(n_pieces, moves, absolute, pinned, where_ref, *refs):
    n_acts = 1 if pinned else 8
    act_refs, src, rest = refs[:n_acts], refs[n_acts : n_acts + n_pieces], refs[n_acts + n_pieces :]
    n_out = 1 if absolute else 4
    outs, rest = rest[:n_out], rest[n_out:]
    if pinned:
        weight, result, sems = rest
        acts = act_refs[0]
    else:
        acts, weight, result, sems, act_sems = rest
    y, x, c = where_ref[0], where_ref[2], where_ref[3]
    act_copies = []
    for k in range(0 if pinned else 8):
        core = c if k < 4 else 1 - c
        chip = lax.rem(x + 4 + (0, 2 * core - 1, 1 - 2 * core, 2)[k % 4], 4)
        block = lax.rem(chip, 2) * 2 + core
        view = act_refs[k]
        target = acts.at[chip // 2, :, pl.ds(pl.multiple_of(block * CH, CH), CH)]
        act_copies.append(pltpu.make_async_copy(view, target, act_sems.at[chip // 2, block]))
    copies = []
    for n, (piece, row, col, kind) in enumerate(moves):
        start = pl.multiple_of(k_block(y, kind) * CH, CH)
        target = weight.at[pl.ds(start, CH), pl.ds(col * 128, 128)]
        copies.append(pltpu.make_async_copy(src[piece].at[pl.ds(row, CH)], target, sems.at[n]))
    for copy in act_copies[:1] + act_copies[4:5] + copies + act_copies[1:4] + act_copies[5:]:
        copy.start()
    for copy in copies:
        copy.wait()
    columns = weight.shape[1]
    for turn in range(2):
        half = x // 2 if turn == 0 else 1 - x // 2
        for block in range(0 if pinned else 4):
            view = acts.at[half, :, pl.ds(block * CH, CH)]
            pltpu.make_async_copy(act_refs[0], view, act_sems.at[half, block]).wait()
        rows = pl.ds(pl.multiple_of(half * TOK, TOK), TOK)
        for at in range(0, columns, 256):
            span = slice(at, min(at + 256, columns))
            result[rows, span] = jnp.dot(acts[half], weight[:, span], preferred_element_type=F32).astype(BF16)
    if absolute:
        for device in range(8):
            outs[0][device] = result[device * 128 : (device + 1) * 128]
    else:
        for step in range(4):
            for other in range(2):
                core = c if other == 0 else 1 - c
                row = pl.multiple_of((lax.rem(x + step, 4) * 2 + core) * 128, 128)
                outs[step][other] = result[pl.ds(row, 128), :]


def project(where, acts, pieces, moves, columns, absolute):
    any_space, vmem = pl.BlockSpec(memory_space=pl.ANY), pl.BlockSpec(memory_space=pltpu.VMEM)
    width = columns * 128
    if absolute:
        shapes = [jax.ShapeDtypeStruct((8, 128, width), BF16)]
    else:
        shapes = [jax.ShapeDtypeStruct((2, 128, width), BF16)] * 4
    scratch = [
        pltpu.VMEM((4 * CH, width), BF16),
        pltpu.VMEM((2 * TOK, width), BF16),
        pltpu.SemaphoreType.DMA((len(moves),)),
    ]
    pinned = len(acts) == 1
    if pinned:
        acts = [pltpu.with_memory_space_constraint(acts[0], pltpu.VMEM)]
    else:
        shapes = shapes + [pltpu.VMEM((2, TOK, 4 * CH), BF16)]
        scratch.append(pltpu.SemaphoreType.DMA((2, 4)))
    act_specs = [vmem] if pinned else [any_space] * 8
    return pl.pallas_call(
        functools.partial(project_kernel, len(pieces), moves, absolute, pinned),
        in_specs=[pl.BlockSpec(memory_space=pltpu.SMEM)] + act_specs + [any_space] * len(pieces),
        out_specs=[vmem] * len(shapes),
        out_shape=shapes,
        scratch_shapes=scratch,
        compiler_params=pltpu.CompilerParams(vmem_limit_bytes=(40 if pinned else 52) << 20),
        cost_estimate=pl.CostEstimate(flops=2 * 1024 * 4096 * width, bytes_accessed=12 << 20, transcendentals=0),
    )(where, *acts, *pieces)


def assemble_kernel(where_ref, *refs):
    out_ref = refs[-1]
    z, x, c = where_ref[1], where_ref[2], where_ref[3]

    def put(chip, core, columns, value):
        base = ((lax.rem(chip, 2) * 2 + core) * 2 + chip // 2) * 8
        for e, i in enumerate(columns):
            col = pl.multiple_of((base + lax.rem(z + i, 8)) * 128, 128)
            out_ref[:, pl.ds(col, 128)] = value[:, e * 128 : (e + 1) * 128]

    for chunk, columns in enumerate(CHUNKS[:-1]):
        parts = refs[chunk * 5 : chunk * 5 + 5]
        for step in range(4):
            chip = lax.rem(x + 4 - step, 4)
            put(chip, c, columns, parts[step][0])
            put(chip, 1 - c, columns, parts[4][step])
    for device in range(8):
        put(jnp.int32(device // 2), device % 2, CHUNKS[-1], refs[-2][device])


def assemble(where, parts):
    vmem = pl.BlockSpec(memory_space=pltpu.VMEM)
    return pl.pallas_call(
        assemble_kernel,
        in_specs=[pl.BlockSpec(memory_space=pltpu.SMEM)] + [vmem] * len(parts),
        out_specs=vmem,
        out_shape=jax.ShapeDtypeStruct((TOK // 4, 8 * CH), BF16),
        compiler_params=pltpu.CompilerParams(vmem_limit_bytes=24 << 20),
        cost_estimate=pl.CostEstimate(flops=0, bytes_accessed=4 << 20, transcendentals=0),
    )(where, *parts)


def shift(value, axis, steps):
    size = lax.axis_size(axis)
    return lax.ppermute(value, axis, [(i, (i + steps) % size) for i in range(size)])


def opposite(value, axis, size, first):
    pairs = [(2 * i + c, 2 * ((i + (first if c == 0 else -first)) % size) + c) for i in range(size) for c in range(2)]
    return lax.ppermute(value, (axis, "c") if isinstance(axis, str) else axis + ("c",), pairs)


def exchange(value, kind):
    held = [(d % 2) * 2 + (1 - d // 2 if kind else d // 2) for d in range(4)]
    pairs = [(a * 4 + b, held.index(b) * 4 + a) for a in range(4) for b in range(4)]
    return lax.ppermute(value, ("y", "xl", "c"), pairs)


def swap_cores(value):
    return lax.ppermute(value, "c", [(0, 1), (1, 0)])


def together(*values):
    return lax.optimization_barrier(values)


RING = ("xh", "xl")


def on_device(projected, short_taps, filter_taps, decay_rates, bypass_gain, out_weight):
    chip = lax.axis_index("xh") * 2 + lax.axis_index("xl")
    where = jnp.stack([lax.axis_index("y"), lax.axis_index("z"), chip, lax.axis_index("c")]).astype(jnp.int32)

    places = {i: [] for i in range(8)}
    buffers = []
    column = {}

    def keep_column(i, buffer):
        column[i] = buffer
        places[i] += [(len(buffers), 0, 0), (len(buffers), CH, 1)]
        buffers.append(buffer)

    def along_y(*columns):
        rows = [column[i][:CH] for i in columns]
        rows = rows[0] if len(rows) == 1 else jnp.concatenate(rows)
        return shift(rows, "y", -1), shift(rows, "y", 1)

    def keep_rows(columns, *both):
        for kind, buffer in zip((2, 3), both, strict=True):
            for e, i in enumerate(columns):
                places[i].append((len(buffers), e * CH, kind))
            buffers.append(buffer)

    def work_on(columns, acts, absolute):
        used, moves = [], []
        for col, i in enumerate(columns):
            for n, row, kind in places[i]:
                if n not in used:
                    used.append(n)
                moves.append((used.index(n), row, col, kind))
        return project(where, acts, [buffers[n] for n in used], tuple(moves), len(columns), absolute)

    def to_cell(sent):
        return [shift(sent[step], RING, step) for step in (1, 2, 3)]

    def other_cores(got):
        return swap_cores(jnp.stack([g[1] for g in got]))

    x = jnp.transpose(projected, (1, 0, 2))
    tail = tail_rows(x, short_taps)
    halo = lax.ppermute(tail, ("y", "xh", "z"), [(i, i + 1) for i in range(63)])
    blocks = [exchange(out_weight, 0), exchange(out_weight, 1)]
    gated = mixer(x, halo, short_taps, filter_taps, decay_rates, bypass_gain)
    *blocks, gated = together(*blocks, gated)
    keep_column(0, jnp.concatenate(blocks))
    one = opposite(gated, RING, 4, 1)
    first, last, *rows, one = together(shift(column[0], "z", -1), shift(column[0], "z", 1), *along_y(0), one)
    keep_column(1, first)
    keep_column(7, last)
    keep_rows((0,), *rows)
    two = opposite(together(gated, first)[0], RING, 4, -1)
    first, last, *rows, two = together(shift(column[1], "z", -1), shift(column[7], "z", 1), *along_y(1, 7), two)
    keep_column(2, first)
    keep_column(6, last)
    keep_rows((1, 7), *rows)
    three = opposite(together(one, first)[0], RING, 4, 1)
    first, last, *rows, three = together(shift(column[2], "z", -1), shift(column[6], "z", 1), *along_y(2, 6), three)
    keep_column(3, first)
    keep_column(5, last)
    keep_rows((2, 6), *rows)
    own, one, two, three, _ = together(gated, one, two, three, first)
    acts = [own, one, two, three] + [swap_cores(v) for v in (own, one, two, three)]
    *sent, held = work_on(CHUNKS[0], acts, False)
    middle, *rows = together(shift(column[3], "z", -1), *along_y(3, 5), *sent)
    rows, sent = rows[:2], rows[2:]
    keep_column(4, middle)
    keep_rows((3, 5), *rows)
    own_0, got_0 = sent[0], to_cell(sent)
    rows = together(*along_y(4))
    keep_rows((4,), *rows)
    (last_sent,) = work_on(CHUNKS[1], [held], True)
    *got_0, last_sent = together(*got_0, last_sent)
    swapped_0 = other_cores([own_0] + got_0)
    last_got = lax.all_to_all(last_sent, RING + ("c",), 0, 0, tiled=True)
    return assemble(where, [own_0, *got_0, swapped_0, last_got])


def solution(mesh):
    fine = Mesh(mesh.devices.reshape(4, 2, 8, 2, 2), ("y", "xh", "z", "xl", "c"))
    ctx, tp = ("y", "xh", "z"), ("xl", "c")
    return jax.shard_map(
        on_device,
        mesh=fine,
        in_specs=(P(ctx, None, tp), P(None, None, tp), P(tp, None), P(tp), P(tp), P(tp, ctx)),
        out_specs=P(ctx + tp, None),
        check_vma=False,
    )
```

time: 190 us -> 144 us (0.76)
  blocking collectives: 37.4 us -> 0 us
  waiting for transfers between devices: 43.7 us -> 63.9 us
  local copies, waits for them, and re-layouts: 18.1 us -> 1.92 us
  between operations: 13.6 us -> 0.28 us
  Pallas kernels: 24.9 us -> 34 us
  starting transfers between devices: 50.8 us -> 43.1 us
    all_to_all x1 -> x0, blocking collectives: 37.4 us -> none  [on_device(): got = lax.all_to_all(mine.reshape(8, TOK // 4, CH), CELL, 0, 0, tiled=True)]
    ppermute x24 -> x20, starting transfers between devices: 33.7 us -> 18.2 us  [shift(): lax.ppermute(value, axis, [(i, (i + steps) % size) for i in range(size)])]
    ppermute x1 -> x10, waiting for transfers between devices: 5.14 us -> 16.2 us  [the longest x2 8.58 us: exchange(): return lax.ppermute(value, ('y', 'xl', 'c'), pairs)]
    all_to_all x0 -> x1, waiting for transfers between devices: none -> 10 us  [on_device(): last_got = lax.all_to_all(last_sent, RING + ('c',), 0, 0, tiled=True)]
    pallas_call x2 -> x4, Pallas kernels: 18.7 us -> 26.8 us  [the longest x2 22.3 us: project(): pl.pallas_call(functools.partial(project_kernel, len(pieces), moves, abso...]
    unnamed x40 -> x31, local copies, waits for them, and re-layouts: 8.78 us -> 0.78 us
    all_to_all x0 -> x1, starting transfers between devices: none -> 5.36 us  [on_device(): last_got = lax.all_to_all(last_sent, RING + ('c',), 0, 0, tiled=True)]
    reshape x2 -> x0, local copies, waits for them, and re-layouts: 4.98 us -> none  [the longest x1 2.8 us: on_device(): return jnp.transpose(got, (2, 1, 0, 3)).reshape(TOK // 4, 8 * CH)]
  transfers between devices with their start and end apart: 27 -> 32, of which waited for: 10 -> 23; matrix products, arithmetic and copies ran while one was open for 2% -> 1% of each run, Pallas kernels for 0% -> 20%
where the time goes in v2:
time: 144 us
  waiting for transfers between devices  63.9 us (44%)
  starting transfers between devices  43.1 us (30%)
  Pallas kernels  34 us (24%)
  local copies, waits for them, and re-layouts  1.92 us (1%)
    ppermute x20, waiting for transfers between devices, shift(): lax.ppermute(value, axis, [(i, (i + steps) % size) for i in range(size)])  37.5 us
    pallas_call x2, Pallas kernels, project(): pl.pallas_call(functools.partial(project_kernel, len(pieces), moves, abso...  22.3 us
    ppermute x20, starting transfers between devices, shift(): lax.ppermute(value, axis, [(i, (i + steps) % size) for i in range(size)])  18.2 us
    all_to_all x1, waiting for transfers between devices, on_device(): last_got = lax.all_to_all(last_sent, RING + ('c',), 0, 0, tiled=True)  10 us
    ppermute x2, waiting for transfers between devices, exchange(): return lax.ppermute(value, ('y', 'xl', 'c'), pairs)  8.58 us
    pallas_call x1, Pallas kernels, mixer(): pl.pallas_call(mixer_kernel, grid=(steps,), in_specs=[pl.BlockSpec((3, TO...  7.23 us
    ppermute x2, starting transfers between devices, exchange(): return lax.ppermute(value, ('y', 'xl', 'c'), pairs)  5.74 us
    all_to_all x1, starting transfers between devices, on_device(): last_got = lax.all_to_all(last_sent, RING + ('c',), 0, 0, tiled=True)  5.36 us
  transfers between devices with their start and end apart: 32, of which 23 were waited for; matrix products, arithmetic and copies ran while one was open for 1% of the time, Pallas kernels for 20%

profile of v2, /device:TPU:1, one launch (start us, length us, event | category | flops | bytes accessed | tf_op | source)
XLA Modules:
  0.0 144.1 jit_solution(15948617290032725351)
XLA Ops:
  0.0 2.2 %shard_map.82 = bf16[144,1024]{1,0:T(8,128)(2,1)} custom-call(bf16[3,512,1024]{2,1,0:T(8,128)(2,1)} %bitcast.7, bf16[3,512,1024]{2,1,0:T(8,128)(2,1)} %bitcast.8, f32[3,3,1024]{2,1,0:T(4,128)} %taps_ref.3), custom_call_target="tpu_custom_call" | custom-call | flops 524288 | bytes 2097152 | tf_op jit(solution)/shard_map/pallas_call | solution.py:74
  2.2 4.4 %collective-permute-start.2 = (bf16[144,1024]{1,0:T(8,128)(2,1)}, bf16[144,1024]{1,0:T(8,128)(2,1)S(1)}, u32[]{:S(2)}, u32[]{:S(2)}) collective-permute-start(bf16[144,1024]{1,0:T(8,128)(2,1)} %shard_map.82), channel_id=1, source_target_pairs={{0,4},{4,8},{8,12},{12,16},{16,20},{20,24},{24,28},{28,32},{32,36}... | collective-permute-start | bytes 884744 | tf_op jit(solution)/shard_map/ppermute | solution.py:342
  6.6 5.6 %collective-permute-start = (bf16[1024,128]{1,0:T(8,128)(2,1)S(1)}, bf16[1024,128]{1,0:T(8,128)(2,1)S(1)}, u32[]{:S(2)}, u32[]{:S(2)}) collective-permute-start(bf16[1024,128]{1,0:T(8,128)(2,1)S(1)} %copy-done.12), channel_id=1, source_target_pairs={{0,0},{1,128},{2,64},{3,192},{64,1},{65,129},{66,65},{67,193},{128... | collective-permute-start | bytes 786440 | tf_op jit(solution)/shard_map/ppermute | solution.py:287
  13.2 7.2 %shard_map.83.refs_0_ = bf16[512,1024]{1,0:T(8,128)(2,1)} custom-call(bf16[3,512,1024]{2,1,0:T(8,128)(2,1)} %bitcast.9, bf16[144,1024]{1,0:T(8,128)(2,1)} %copy-done.11, f32[3,3,1024]{2,1,0:T(4,128)} %taps_ref.3, f32[1024,128]{1,0:T(8,128)} %filt_ref.1, f32[1,1024]{1,0:T(1,128)} %bitcast.10, f32[1,1024]{1,0:T(1,128)} %bitcast.11, ...), custom_call_target="tpu_custom_call" | custom-call | flops 1800000000 | bytes 6291456 | tf_op jit(solution)/shard_map/pallas_call | solution.py:133
  20.5 8.6 %collective-permute-done = bf16[1024,128]{1,0:T(8,128)(2,1)S(1)} collective-permute-done((bf16[1024,128]{1,0:T(8,128)(2,1)S(1)}, bf16[1024,128]{1,0:T(8,128)(2,1)S(1)}, u32[]{:S(2)}, u32[]{:S(2)}) %collective-permute-start) | collective-permute-done | bytes 262176 | tf_op jit(solution)/shard_map/ppermute | solution.py:287
  29.1 2.0 %collective-permute-start.7 = (bf16[512,1024]{1,0:T(8,128)(2,1)}, bf16[512,1024]{1,0:T(8,128)(2,1)}, u32[]{:S(2)}, u32[]{:S(2)}) collective-permute-start(bf16[512,1024]{1,0:T(8,128)(2,1)} %shard_map.83.refs_0_), channel_id=1, source_target_pairs={{0,2},{1,35},{2,32},{3,1},{32,34},{33,3},{34,0},{35,33},{4,6},{5,3... | collective-permute-start | bytes 3145736 | tf_op jit(solution)/shard_map/ppermute | solution.py:281
  34.4 3.8 %collective-permute-done.5.refs_9_ = bf16[1024,128]{1,0:T(8,128)(2,1)S(1)} collective-permute-done((bf16[1024,128]{1,0:T(8,128)(2,1)S(1)}, bf16[1024,128]{1,0:T(8,128)(2,1)S(1)}, u32[]{:S(2)}, u32[]{:S(2)}) %collective-permute-start.5) | collective-permute-done | bytes 262176 | tf_op jit(solution)/shard_map/ppermute | solution.py:276
  38.3 3.1 %collective-permute-done.6.refs_10_ = bf16[1024,128]{1,0:T(8,128)(2,1)S(1)} collective-permute-done((bf16[1024,128]{1,0:T(8,128)(2,1)S(1)}, bf16[1024,128]{1,0:T(8,128)(2,1)S(1)}, u32[]{:S(2)}, u32[]{:S(2)}) %collective-permute-start.6) | collective-permute-done | bytes 262176 | tf_op jit(solution)/shard_map/ppermute | solution.py:276
  41.7 2.1 %collective-permute-done.4.refs_14_ = bf16[2048,128]{1,0:T(8,128)(2,1)S(1)} collective-permute-done((bf16[2048,128]{1,0:T(8,128)(2,1)S(1)}, bf16[2048,128]{1,0:T(8,128)(2,1)S(1)}, u32[]{:S(2)}, u32[]{:S(2)}) %collective-permute-start.4) | collective-permute-done | bytes 524320 | tf_op jit(solution)/shard_map/ppermute | solution.py:276
  50.1 7.3 %collective-permute-done.10.refs_12_ = bf16[2048,128]{1,0:T(8,128)(2,1)S(1)} collective-permute-done((bf16[2048,128]{1,0:T(8,128)(2,1)S(1)}, bf16[2048,128]{1,0:T(8,128)(2,1)S(1)}, u32[]{:S(2)}, u32[]{:S(2)}) %collective-permute-start.10) | collective-permute-done | bytes 524320 | tf_op jit(solution)/shard_map/ppermute | solution.py:276
  60.9 1.9 %collective-permute-start.17 = (bf16[512,1024]{1,0:T(8,128)(2,1)}, bf16[512,1024]{1,0:T(8,128)(2,1)}, u32[]{:S(2)}, u32[]{:S(2)}) collective-permute-start(bf16[512,1024]{1,0:T(8,128)(2,1)} %collective-permute-done.7.refs_1_), channel_id=1, source_target_pairs={{0,2},{1,35},{2,32},{3,1},{32,34},{33,3},{34,0},{35,33},{4,6},{5,3... | collective-permute-start | bytes 3145736 | tf_op jit(solution)/shard_map/ppermute | solution.py:281
  62.8 1.9 %collective-permute-start.15 = (bf16[2048,128]{1,0:T(8,128)(2,1)S(1)}, bf16[2048,128]{1,0:T(8,128)(2,1)S(1)}, u32[]{:S(2)}, u32[]{:S(2)}) collective-permute-start(bf16[2048,128]{1,0:T(8,128)(2,1)S(1)} %pad_maximum_fusion.2), channel_id=1, source_target_pairs={{0,192},{64,0},{128,64},{192,128},{1,193},{65,1},{129,65},{193,129... | collective-permute-start | bytes 1572872 | tf_op jit(solution)/shard_map/ppermute | solution.py:276
  66.4 8.0 %collective-permute-done.15.refs_16_ = bf16[2048,128]{1,0:T(8,128)(2,1)S(1)} collective-permute-done((bf16[2048,128]{1,0:T(8,128)(2,1)S(1)}, bf16[2048,128]{1,0:T(8,128)(2,1)S(1)}, u32[]{:S(2)}, u32[]{:S(2)}) %collective-permute-start.15) | collective-permute-done | bytes 524320 | tf_op jit(solution)/shard_map/ppermute | solution.py:276
  75.9 2.6 %collective-permute-done.14.refs_4_ = bf16[2048,128]{1,0:T(8,128)(2,1)S(1)} collective-permute-done((bf16[2048,128]{1,0:T(8,128)(2,1)S(1)}, bf16[2048,128]{1,0:T(8,128)(2,1)S(1)}, u32[]{:S(2)}, u32[]{:S(2)}) %collective-permute-start.14) | collective-permute-done | bytes 524320 | tf_op jit(solution)/shard_map/ppermute | solution.py:276
  78.5 3.4 %collective-permute-start.21 = (bf16[512,1024]{1,0:T(8,128)(2,1)}, bf16[512,1024]{1,0:T(8,128)(2,1)}, u32[]{:S(2)}, u32[]{:S(2)}) collective-permute-start(bf16[512,1024]{1,0:T(8,128)(2,1)} %shard_map.83.refs_0_), channel_id=1, source_target_pairs={{0,1},{1,0},{2,3},{3,2},{4,5},{5,4},{6,7},{7,6},{8,9},{9,8},{10,11... | collective-permute-start | bytes 3145736 | tf_op jit(solution)/shard_map/ppermute | solution.py:291
  89.0 15.6 %shard_map.84 = (bf16[2,128,640]{2,1,0:T(8,128)(2,1)}, bf16[2,128,640]{2,1,0:T(8,128)(2,1)}, bf16[2,128,640]{2,1,0:T(8,128)(2,1)}, bf16[2,128,640]{2,1,0:T(8,128)(2,1)}, bf16[2,512,4096]{2,1,0:T(8,128)(2,1)S(1)}) custom-call(s32[4]{0:T(128)} %pad_add_fusion.where_ref, bf16[512,1024]{1,0:T(8,128)(2,1)} %shard_map.83.refs_0_, ...), custom_call_target="tpu_custom_call" | custom-call | flops 5368709120 | bytes 12582912 | tf_op jit(solution)/shard_map/pallas_call | solution.py:231
  106.3 2.5 %collective-permute-start.26 = (bf16[2,128,640]{2,1,0:T(8,128)(2,1)}, bf16[2,128,640]{2,1,0:T(8,128)(2,1)S(1)}, u32[]{:S(2)}, u32[]{:S(2)}) collective-permute-start(bf16[2,128,640]{2,1,0:T(8,128)(2,1)} %get-tuple-element.77), channel_id=1, source_target_pairs={{0,32},{2,34},{32,0},{34,2},{1,33},{3,35},{33,1},{35,3},{4,36},{6,... | collective-permute-start | bytes 983048 | tf_op jit(solution)/shard_map/ppermute | solution.py:276
  110.7 2.0 %collective-permute-done.28.refs_6_ = bf16[1024,128]{1,0:T(8,128)(2,1)S(1)} collective-permute-done((bf16[1024,128]{1,0:T(8,128)(2,1)S(1)}, bf16[1024,128]{1,0:T(8,128)(2,1)S(1)}, u32[]{:S(2)}, u32[]{:S(2)}) %collective-permute-start.28) | collective-permute-done | bytes 262176 | tf_op jit(solution)/shard_map/ppermute | solution.py:276
  112.7 2.4 %collective-permute-done.29.refs_7_ = bf16[1024,128]{1,0:T(8,128)(2,1)S(1)} collective-permute-done((bf16[1024,128]{1,0:T(8,128)(2,1)S(1)}, bf16[1024,128]{1,0:T(8,128)(2,1)S(1)}, u32[]{:S(2)}, u32[]{:S(2)}) %collective-permute-start.29) | collective-permute-done | bytes 262176 | tf_op jit(solution)/shard_map/ppermute | solution.py:276
  115.2 6.7 %shard_map.85 = bf16[8,128,384]{2,1,0:T(8,128)(2,1)} custom-call(s32[4]{0:T(128)S(1)} %copy-done.1, bf16[2,512,4096]{2,1,0:T(8,128)(2,1)S(1)} %get-tuple-element.79.refs_0_, bf16[2048,128]{1,0:T(8,128)(2,1)S(1)} %collective-permute-done.13.refs_1_, bf16[2048,128]{1,0:T(8,128)(2,1)S(1)} %collective-permute-done.19.refs_2_, ...), custom_call_target="tpu_custom_call" | custom-call | flops 3221225472 | bytes 12582912 | tf_op jit(solution)/shard_map/pallas_call | solution.py:231
  124.1 5.4 %all-to-all-start = ((bf16[8,128,384]{2,1,0:T(8,128)(2,1)}), bf16[8,128,384]{2,1,0:T(8,128)(2,1)S(1)}, u32[]{:S(2)}, u32[]{:S(2)}) async-start(bf16[8,128,384]{2,1,0:T(8,128)(2,1)} %shard_map.85), calls=%async_computation | async-start | bytes 1572864 | tf_op jit(solution)/shard_map/all_to_all | solution.py:375
  129.7 2.1 %collective-permute-done.30.refs_4_ = bf16[4,128,640]{2,1,0:T(8,128)(2,1)S(1)} collective-permute-done((bf16[4,128,640]{2,1,0:T(8,128)(2,1)S(1)}, bf16[4,128,640]{2,1,0:T(8,128)(2,1)S(1)}, u32[]{:S(2)}, u32[]{:S(2)}) %collective-permute-start.30) | collective-permute-done | bytes 655392 | tf_op jit(solution)/shard_map/ppermute | solution.py:291
  131.8 10.0 %all-to-all-done.refs_5_ = bf16[8,128,384]{2,1,0:T(8,128)(2,1)S(1)} async-done(((bf16[8,128,384]{2,1,0:T(8,128)(2,1)}), bf16[8,128,384]{2,1,0:T(8,128)(2,1)S(1)}, u32[]{:S(2)}, u32[]{:S(2)}) %all-to-all-start) | async-done | bytes 786464 | tf_op jit(solution)/shard_map/all_to_all | solution.py:375
  141.8 2.3 %shard_map.86 = bf16[128,8192]{1,0:T(8,128)(2,1)} custom-call(s32[4]{0:T(128)S(1)} %copy-done.1, bf16[2,128,640]{2,1,0:T(8,128)(2,1)S(1)} %copy-done, bf16[2,128,640]{2,1,0:T(8,128)(2,1)S(1)} %collective-permute-done.25.refs_1_, bf16[2,128,640]{2,1,0:T(8,128)(2,1)S(1)} %collective-permute-done.26.refs_2_, ...), custom_call_target="tpu_custom_call" | custom-call | bytes 4194304 | tf_op jit(solution)/shard_map/pallas_call | solution.py:264
  (93 shorter events, 30.7 us)
Async XLA Ops:
  2.2 10.3 %collective-permute-start.2 = (bf16[144,1024]{1,0:T(8,128)(2,1)}, bf16[144,1024]{1,0:T(8,128)(2,1)S(1)}, u32[]{:S(2)}, u32[]{:S(2)}) collective-permute-start(bf16[144,1024]{1,0:T(8,128)(2,1)} %shard_map.82), channel_id=1, source_target_pairs={{0,4},{4,8},{8,12},{12,16},{16,20},{20,24},{24,28},{28,32},{32,36}... | collective-permute-start | bytes 884744 | tf_op jit(solution)/shard_map/ppermute | solution.py:342
  6.6 22.5 %collective-permute-start = (bf16[1024,128]{1,0:T(8,128)(2,1)S(1)}, bf16[1024,128]{1,0:T(8,128)(2,1)S(1)}, u32[]{:S(2)}, u32[]{:S(2)}) collective-permute-start(bf16[1024,128]{1,0:T(8,128)(2,1)S(1)} %copy-done.12), channel_id=1, source_target_pairs={{0,0},{1,128},{2,64},{3,192},{64,1},{65,129},{66,65},{67,193},{128... | collective-permute-start | bytes 786440 | tf_op jit(solution)/shard_map/ppermute | solution.py:287
  12.2 16.8 %collective-permute-start.1 = (bf16[1024,128]{1,0:T(8,128)(2,1)S(1)}, bf16[1024,128]{1,0:T(8,128)(2,1)S(1)}, u32[]{:S(2)}, u32[]{:S(2)}) collective-permute-start(bf16[1024,128]{1,0:T(8,128)(2,1)S(1)} %copy-done.12), channel_id=1, source_target_pairs={{0,128},{1,0},{2,192},{3,64},{64,129},{65,1},{66,193},{67,65},{128... | collective-permute-start | bytes 786440 | tf_op jit(solution)/shard_map/ppermute | solution.py:287
  29.1 16.4 %collective-permute-start.7 = (bf16[512,1024]{1,0:T(8,128)(2,1)}, bf16[512,1024]{1,0:T(8,128)(2,1)}, u32[]{:S(2)}, u32[]{:S(2)}) collective-permute-start(bf16[512,1024]{1,0:T(8,128)(2,1)} %shard_map.83.refs_0_), channel_id=1, source_target_pairs={{0,2},{1,35},{2,32},{3,1},{32,34},{33,3},{34,0},{35,33},{4,6},{5,3... | collective-permute-start | bytes 3145736 | tf_op jit(solution)/shard_map/ppermute | solution.py:281
  31.1 10.6 %collective-permute-start.3 = (bf16[2048,128]{1,0:T(8,128)(2,1)S(1)}, bf16[2048,128]{1,0:T(8,128)(2,1)S(1)}, u32[]{:S(2)}, u32[]{:S(2)}) collective-permute-start(bf16[2048,128]{1,0:T(8,128)(2,1)S(1)} %constant_dynamic-update-slice_fusion.refs_8_), channel_id=1, source_target_pairs={{0,28},{4,0},{8,4},{12,8},{16,12},{20,16},{24,20},{28,24},{1,29},{... | collective-permute-start | bytes 1572872 | tf_op jit(solution)/shard_map/ppermute | solution.py:276
  31.7 12.1 %collective-permute-start.4 = (bf16[2048,128]{1,0:T(8,128)(2,1)S(1)}, bf16[2048,128]{1,0:T(8,128)(2,1)S(1)}, u32[]{:S(2)}, u32[]{:S(2)}) collective-permute-start(bf16[2048,128]{1,0:T(8,128)(2,1)S(1)} %constant_dynamic-update-slice_fusion.refs_8_), channel_id=1, source_target_pairs={{0,4},{4,8},{8,12},{12,16},{16,20},{20,24},{24,28},{28,0},{1,5},{5... | collective-permute-start | bytes 1572872 | tf_op jit(solution)/shard_map/ppermute | solution.py:276
  45.5 15.4 %collective-permute-start.12 = (bf16[512,1024]{1,0:T(8,128)(2,1)}, bf16[512,1024]{1,0:T(8,128)(2,1)}, u32[]{:S(2)}, u32[]{:S(2)}) collective-permute-start(bf16[512,1024]{1,0:T(8,128)(2,1)} %shard_map.83.refs_0_), channel_id=1, source_target_pairs={{0,34},{1,3},{2,0},{3,33},{32,2},{33,35},{34,32},{35,1},{4,38},{5,... | collective-permute-start | bytes 3145736 | tf_op jit(solution)/shard_map/ppermute | solution.py:281
  47.0 10.4 %collective-permute-start.10 = (bf16[2048,128]{1,0:T(8,128)(2,1)S(1)}, bf16[2048,128]{1,0:T(8,128)(2,1)S(1)}, u32[]{:S(2)}, u32[]{:S(2)}) collective-permute-start(bf16[2048,128]{1,0:T(8,128)(2,1)S(1)} %pad_maximum_fusion.1), channel_id=1, source_target_pairs={{0,192},{64,0},{128,64},{192,128},{1,193},{65,1},{129,65},{193,129... | collective-permute-start | bytes 1572872 | tf_op jit(solution)/shard_map/ppermute | solution.py:276
  47.9 10.5 %collective-permute-start.11 = (bf16[2048,128]{1,0:T(8,128)(2,1)S(1)}, bf16[2048,128]{1,0:T(8,128)(2,1)S(1)}, u32[]{:S(2)}, u32[]{:S(2)}) collective-permute-start(bf16[2048,128]{1,0:T(8,128)(2,1)S(1)} %pad_maximum_fusion.1), channel_id=1, source_target_pairs={{0,64},{64,128},{128,192},{192,0},{1,65},{65,129},{129,193},{193,1... | collective-permute-start | bytes 1572872 | tf_op jit(solution)/shard_map/ppermute | solution.py:276
  48.6 9.8 %collective-permute-start.8 = (bf16[2048,128]{1,0:T(8,128)(2,1)S(1)}, bf16[2048,128]{1,0:T(8,128)(2,1)S(1)}, u32[]{:S(2)}, u32[]{:S(2)}) collective-permute-start(bf16[2048,128]{1,0:T(8,128)(2,1)S(1)} %collective-permute-done.3.refs_11_), channel_id=1, source_target_pairs={{0,28},{4,0},{8,4},{12,8},{16,12},{20,16},{24,20},{28,24},{1,29},{... | collective-permute-start | bytes 1572872 | tf_op jit(solution)/shard_map/ppermute | solution.py:276
  48.6 10.8 %collective-permute-start.9 = (bf16[2048,128]{1,0:T(8,128)(2,1)S(1)}, bf16[2048,128]{1,0:T(8,128)(2,1)S(1)}, u32[]{:S(2)}, u32[]{:S(2)}) collective-permute-start(bf16[2048,128]{1,0:T(8,128)(2,1)S(1)} %collective-permute-done.4.refs_14_), channel_id=1, source_target_pairs={{0,4},{4,8},{8,12},{12,16},{16,20},{20,24},{24,28},{28,0},{1,5},{5... | collective-permute-start | bytes 1572872 | tf_op jit(solution)/shard_map/ppermute | solution.py:276
  60.9 17.7 %collective-permute-start.17 = (bf16[512,1024]{1,0:T(8,128)(2,1)}, bf16[512,1024]{1,0:T(8,128)(2,1)}, u32[]{:S(2)}, u32[]{:S(2)}) collective-permute-start(bf16[512,1024]{1,0:T(8,128)(2,1)} %collective-permute-done.7.refs_1_), channel_id=1, source_target_pairs={{0,2},{1,35},{2,32},{3,1},{32,34},{33,3},{34,0},{35,33},{4,6},{5,3... | collective-permute-start | bytes 3145736 | tf_op jit(solution)/shard_map/ppermute | solution.py:281
  62.8 11.6 %collective-permute-start.15 = (bf16[2048,128]{1,0:T(8,128)(2,1)S(1)}, bf16[2048,128]{1,0:T(8,128)(2,1)S(1)}, u32[]{:S(2)}, u32[]{:S(2)}) collective-permute-start(bf16[2048,128]{1,0:T(8,128)(2,1)S(1)} %pad_maximum_fusion.2), channel_id=1, source_target_pairs={{0,192},{64,0},{128,64},{192,128},{1,193},{65,1},{129,65},{193,129... | collective-permute-start | bytes 1572872 | tf_op jit(solution)/shard_map/ppermute | solution.py:276
  64.8 11.1 %collective-permute-start.16 = (bf16[2048,128]{1,0:T(8,128)(2,1)S(1)}, bf16[2048,128]{1,0:T(8,128)(2,1)S(1)}, u32[]{:S(2)}, u32[]{:S(2)}) collective-permute-start(bf16[2048,128]{1,0:T(8,128)(2,1)S(1)} %pad_maximum_fusion.2), channel_id=1, source_target_pairs={{0,64},{64,128},{128,192},{192,0},{1,65},{65,129},{129,193},{193,1... | collective-permute-start | bytes 1572872 | tf_op jit(solution)/shard_map/ppermute | solution.py:276
  64.9 11.0 %collective-permute-start.13 = (bf16[2048,128]{1,0:T(8,128)(2,1)S(1)}, bf16[2048,128]{1,0:T(8,128)(2,1)S(1)}, u32[]{:S(2)}, u32[]{:S(2)}) collective-permute-start(bf16[2048,128]{1,0:T(8,128)(2,1)S(1)} %collective-permute-done.8.refs_15_), channel_id=1, source_target_pairs={{0,28},{4,0},{8,4},{12,8},{16,12},{20,16},{24,20},{28,24},{1,29},{... | collective-permute-start | bytes 1572872 | tf_op jit(solution)/shard_map/ppermute | solution.py:276
  65.3 13.2 %collective-permute-start.14 = (bf16[2048,128]{1,0:T(8,128)(2,1)S(1)}, bf16[2048,128]{1,0:T(8,128)(2,1)S(1)}, u32[]{:S(2)}, u32[]{:S(2)}) collective-permute-start(bf16[2048,128]{1,0:T(8,128)(2,1)S(1)} %collective-permute-done.9.refs_18_), channel_id=1, source_target_pairs={{0,4},{4,8},{8,12},{12,16},{16,20},{20,24},{24,28},{28,0},{1,5},{5... | collective-permute-start | bytes 1572872 | tf_op jit(solution)/shard_map/ppermute | solution.py:276
  82.7 22.0 %collective-permute-start.19 = (bf16[2048,128]{1,0:T(8,128)(2,1)S(1)}, bf16[2048,128]{1,0:T(8,128)(2,1)S(1)}, u32[]{:S(2)}, u32[]{:S(2)}) collective-permute-start(bf16[2048,128]{1,0:T(8,128)(2,1)S(1)} %pad_maximum_fusion.3), channel_id=1, source_target_pairs={{0,192},{64,0},{128,64},{192,128},{1,193},{65,1},{129,65},{193,129... | collective-permute-start | bytes 1572872 | tf_op jit(solution)/shard_map/ppermute | solution.py:276
  84.5 20.1 %collective-permute-start.20 = (bf16[2048,128]{1,0:T(8,128)(2,1)S(1)}, bf16[2048,128]{1,0:T(8,128)(2,1)S(1)}, u32[]{:S(2)}, u32[]{:S(2)}) collective-permute-start(bf16[2048,128]{1,0:T(8,128)(2,1)S(1)} %pad_maximum_fusion.3), channel_id=1, source_target_pairs={{0,64},{64,128},{128,192},{192,0},{1,65},{65,129},{129,193},{193,1... | collective-permute-start | bytes 1572872 | tf_op jit(solution)/shard_map/ppermute | solution.py:276
  86.0 18.6 %collective-permute-start.18 = (bf16[2048,128]{1,0:T(8,128)(2,1)S(1)}, bf16[2048,128]{1,0:T(8,128)(2,1)S(1)}, u32[]{:S(2)}, u32[]{:S(2)}) collective-permute-start(bf16[2048,128]{1,0:T(8,128)(2,1)S(1)} %collective-permute-done.13.refs_1_), channel_id=1, source_target_pairs={{0,28},{4,0},{8,4},{12,8},{16,12},{20,16},{24,20},{28,24},{1,29},{... | collective-permute-start | bytes 1572872 | tf_op jit(solution)/shard_map/ppermute | solution.py:276
  106.3 8.8 %collective-permute-start.29 = (bf16[1024,128]{1,0:T(8,128)(2,1)S(1)}, bf16[1024,128]{1,0:T(8,128)(2,1)S(1)}, u32[]{:S(2)}, u32[]{:S(2)}) collective-permute-start(bf16[1024,128]{1,0:T(8,128)(2,1)S(1)} %slice.39), channel_id=1, source_target_pairs={{0,64},{64,128},{128,192},{192,0},{1,65},{65,129},{129,193},{193,1... | collective-permute-start | bytes 786440 | tf_op jit(solution)/shard_map/ppermute | solution.py:276
  106.3 15.5 %collective-permute-start.25 = (bf16[2,128,640]{2,1,0:T(8,128)(2,1)}, bf16[2,128,640]{2,1,0:T(8,128)(2,1)S(1)}, u32[]{:S(2)}, u32[]{:S(2)}) collective-permute-start(bf16[2,128,640]{2,1,0:T(8,128)(2,1)} %get-tuple-element.76), channel_id=1, source_target_pairs={{0,2},{2,32},{32,34},{34,0},{1,3},{3,33},{33,35},{35,1},{4,6},{6,3... | collective-permute-start | bytes 983048 | tf_op jit(solution)/shard_map/ppermute | solution.py:276
  106.3 16.5 %collective-permute-start.26 = (bf16[2,128,640]{2,1,0:T(8,128)(2,1)}, bf16[2,128,640]{2,1,0:T(8,128)(2,1)S(1)}, u32[]{:S(2)}, u32[]{:S(2)}) collective-permute-start(bf16[2,128,640]{2,1,0:T(8,128)(2,1)} %get-tuple-element.77), channel_id=1, source_target_pairs={{0,32},{2,34},{32,0},{34,2},{1,33},{3,35},{33,1},{35,3},{4,36},{6,... | collective-permute-start | bytes 983048 | tf_op jit(solution)/shard_map/ppermute | solution.py:276
  108.8 15.2 %collective-permute-start.27 = (bf16[2,128,640]{2,1,0:T(8,128)(2,1)}, bf16[2,128,640]{2,1,0:T(8,128)(2,1)S(1)}, u32[]{:S(2)}, u32[]{:S(2)}) collective-permute-start(bf16[2,128,640]{2,1,0:T(8,128)(2,1)} %get-tuple-element.78), channel_id=1, source_target_pairs={{0,34},{2,0},{32,2},{34,32},{1,35},{3,1},{33,3},{35,33},{4,38},{6,... | collective-permute-start | bytes 983048 | tf_op jit(solution)/shard_map/ppermute | solution.py:276
  124.1 17.7 %all-to-all-start = ((bf16[8,128,384]{2,1,0:T(8,128)(2,1)}), bf16[8,128,384]{2,1,0:T(8,128)(2,1)S(1)}, u32[]{:S(2)}, u32[]{:S(2)}) async-start(bf16[8,128,384]{2,1,0:T(8,128)(2,1)} %shard_map.85), calls=%async_computation | async-start | bytes 1572864 | tf_op jit(solution)/shard_map/all_to_all | solution.py:375
  (23 other events, 384.7 us)

commit v3 on v2

--- a/solution.py
+++ b/solution.py
@@ -160,9 +160,10 @@
     return lax.rem(y, 2) * 2 + (1 - y // 2 if kind == 1 else y // 2)
 
 
-def project_kernel(n_pieces, moves, absolute, pinned, where_ref, *refs):
+def project_kernel(n_pieces, moves, absolute, pinned, n_before, where_ref, *refs):
     n_acts = 1 if pinned else 8
     act_refs, src, rest = refs[:n_acts], refs[n_acts : n_acts + n_pieces], refs[n_acts + n_pieces :]
+    before, rest = rest[:n_before], rest[n_before:]
     n_out = 1 if absolute else 4
     outs, rest = rest[:n_out], rest[n_out:]
     if pinned:
@@ -199,8 +200,12 @@
             span = slice(at, min(at + 256, columns))
             result[rows, span] = jnp.dot(acts[half], weight[:, span], preferred_element_type=F32).astype(BF16)
     if absolute:
+        kept = 0
+        for ref in before:
+            outs[0][:, :, : ref.shape[2]] = ref[...]
+            kept = ref.shape[2]
         for device in range(8):
-            outs[0][device] = result[device * 128 : (device + 1) * 128]
+            outs[0][device, :, kept:] = result[device * 128 : (device + 1) * 128]
     else:
         for step in range(4):
             for other in range(2):
@@ -209,11 +214,12 @@
                 outs[step][other] = result[pl.ds(row, 128), :]
 
 
-def project(where, acts, pieces, moves, columns, absolute):
+def project(where, acts, pieces, moves, columns, absolute, before=()):
     any_space, vmem = pl.BlockSpec(memory_space=pl.ANY), pl.BlockSpec(memory_space=pltpu.VMEM)
     width = columns * 128
     if absolute:
-        shapes = [jax.ShapeDtypeStruct((8, 128, width), BF16)]
+        kept = sum(v.shape[2] for v in before)
+        shapes = [jax.ShapeDtypeStruct((8, 128, kept + width), BF16)]
     else:
         shapes = [jax.ShapeDtypeStruct((2, 128, width), BF16)] * 4
     scratch = [
@@ -229,14 +235,14 @@
         scratch.append(pltpu.SemaphoreType.DMA((2, 4)))
     act_specs = [vmem] if pinned else [any_space] * 8
     return pl.pallas_call(
-        functools.partial(project_kernel, len(pieces), moves, absolute, pinned),
-        in_specs=[pl.BlockSpec(memory_space=pltpu.SMEM)] + act_specs + [any_space] * len(pieces),
+        functools.partial(project_kernel, len(pieces), moves, absolute, pinned, len(before)),
+        in_specs=[pl.BlockSpec(memory_space=pltpu.SMEM)] + act_specs + [any_space] * len(pieces) + [vmem] * len(before),
         out_specs=[vmem] * len(shapes),
         out_shape=shapes,
         scratch_shapes=scratch,
         compiler_params=pltpu.CompilerParams(vmem_limit_bytes=(40 if pinned else 52) << 20),
         cost_estimate=pl.CostEstimate(flops=2 * 1024 * 4096 * width, bytes_accessed=12 << 20, transcendentals=0),
-    )(where, *acts, *pieces)
+    )(where, *acts, *pieces, *before)
 
 
 def assemble_kernel(where_ref, *refs):
@@ -322,14 +328,14 @@
                 places[i].append((len(buffers), e * CH, kind))
             buffers.append(buffer)
 
-    def work_on(columns, acts, absolute):
+    def work_on(columns, acts, absolute, before=()):
         used, moves = [], []
         for col, i in enumerate(columns):
             for n, row, kind in places[i]:
                 if n not in used:
                     used.append(n)
                 moves.append((used.index(n), row, col, kind))
-        return project(where, acts, [buffers[n] for n in used], tuple(moves), len(columns), absolute)
+        return project(where, acts, [buffers[n] for n in used], tuple(moves), len(columns), absolute, before)
 
     def to_cell(sent):
         return [shift(sent[step], RING, step) for step in (1, 2, 3)]
@@ -367,10 +373,9 @@
     keep_column(4, middle)
     keep_rows((3, 5), *rows)
     own_0, got_0 = sent[0], to_cell(sent)
-    rows = together(*along_y(4))
+    *rows, early = together(*along_y(4), *work_on(CHUNKS[1][:2], [held], True))
     keep_rows((4,), *rows)
-    (last_sent,) = work_on(CHUNKS[1], [held], True)
-    *got_0, last_sent = together(*got_0, last_sent)
+    (last_sent,) = work_on(CHUNKS[1][2:], [held], True, [early])
     swapped_0 = other_cores([own_0] + got_0)
     last_got = lax.all_to_all(last_sent, RING + ("c",), 0, 0, tiled=True)
     return assemble(where, [own_0, *got_0, swapped_0, last_got])

time: 144 us -> 139 us (0.965)
  waiting for transfers between devices: 63.9 us -> 56 us
    ppermute x20, waiting for transfers between devices: 37.5 us -> 32.1 us  [shift(): lax.ppermute(value, axis, [(i, (i + steps) % size) for i in range(size)])]
    ppermute x5, waiting for transfers between devices: 4.53 us -> 2.45 us  [swap_cores(): return lax.ppermute(value, 'c', [(0, 1), (1, 0)])]
    pallas_call x2 -> x3, Pallas kernels: 22.3 us -> 22.9 us  [project(): pl.pallas_call(functools.partial(project_kernel, len(pieces), moves, abso...]
  transfers between devices with their start and end apart: 32 -> 32, of which waited for: 23 -> 20; matrix products, arithmetic and copies ran while one was open for 1% -> 2% of each run, Pallas kernels for 20% -> 22%
where the time goes in v3:
time: 139 us; the launch traced here: 138 us
  waiting for transfers between devices  56 us (40%)
  starting transfers between devices  43.8 us (32%)
  Pallas kernels  34.7 us (25%)
  local copies, waits for them, and re-layouts  1.92 us (1%)
  other arithmetic  1.73 us (1%)
    ppermute x20, waiting for transfers between devices, shift(): lax.ppermute(value, axis, [(i, (i + steps) % size) for i in range(size)])  32.1 us
    pallas_call x3, Pallas kernels, project(): pl.pallas_call(functools.partial(project_kernel, len(pieces), moves, abso...  22.9 us
    ppermute x20, starting transfers between devices, shift(): lax.ppermute(value, axis, [(i, (i + steps) % size) for i in range(size)])  18.2 us
    all_to_all x1, waiting for transfers between devices, on_device(): last_got = lax.all_to_all(last_sent, RING + ('c',), 0, 0, tiled=True)  9.63 us
    ppermute x2, waiting for transfers between devices, exchange(): return lax.ppermute(value, ('y', 'xl', 'c'), pairs)  8.58 us
    pallas_call x1, Pallas kernels, mixer(): pl.pallas_call(mixer_kernel, grid=(steps,), in_specs=[pl.BlockSpec((3, TO...  7.23 us
    ppermute x2, starting transfers between devices, exchange(): return lax.ppermute(value, ('y', 'xl', 'c'), pairs)  5.74 us
    ppermute x5, starting transfers between devices, swap_cores(): return lax.ppermute(value, 'c', [(0, 1), (1, 0)])  5.43 us
  transfers between devices with their start and end apart: 32, of which 20 were waited for; matrix products, arithmetic and copies ran while one was open for 2% of the time, Pallas kernels for 22%

profile of v3, /device:TPU:1, one launch (start us, length us, event | category | flops | bytes accessed | tf_op | source)
XLA Modules:
  0.0 138.5 jit_solution(14847077409776385482)
XLA Ops:
  0.0 2.2 %shard_map.82 = bf16[144,1024]{1,0:T(8,128)(2,1)} custom-call(bf16[3,512,1024]{2,1,0:T(8,128)(2,1)} %bitcast.7, bf16[3,512,1024]{2,1,0:T(8,128)(2,1)} %bitcast.8, f32[3,3,1024]{2,1,0:T(4,128)} %taps_ref.3), custom_call_target="tpu_custom_call" | custom-call | flops 524288 | bytes 2097152 | tf_op jit(solution)/shard_map/pallas_call | solution.py:74
  2.2 4.4 %collective-permute-start.2 = (bf16[144,1024]{1,0:T(8,128)(2,1)}, bf16[144,1024]{1,0:T(8,128)(2,1)S(1)}, u32[]{:S(2)}, u32[]{:S(2)}) collective-permute-start(bf16[144,1024]{1,0:T(8,128)(2,1)} %shard_map.82), channel_id=1, source_target_pairs={{0,4},{4,8},{8,12},{12,16},{16,20},{20,24},{24,28},{28,32},{32,36}... | collective-permute-start | bytes 884744 | tf_op jit(solution)/shard_map/ppermute | solution.py:348
  6.6 5.6 %collective-permute-start = (bf16[1024,128]{1,0:T(8,128)(2,1)S(1)}, bf16[1024,128]{1,0:T(8,128)(2,1)S(1)}, u32[]{:S(2)}, u32[]{:S(2)}) collective-permute-start(bf16[1024,128]{1,0:T(8,128)(2,1)S(1)} %copy-done.12), channel_id=1, source_target_pairs={{0,0},{1,128},{2,64},{3,192},{64,1},{65,129},{66,65},{67,193},{128... | collective-permute-start | bytes 786440 | tf_op jit(solution)/shard_map/ppermute | solution.py:293
  13.2 7.2 %shard_map.83.refs_0_ = bf16[512,1024]{1,0:T(8,128)(2,1)} custom-call(bf16[3,512,1024]{2,1,0:T(8,128)(2,1)} %bitcast.9, bf16[144,1024]{1,0:T(8,128)(2,1)} %copy-done.11, f32[3,3,1024]{2,1,0:T(4,128)} %taps_ref.3, f32[1024,128]{1,0:T(8,128)} %filt_ref.1, f32[1,1024]{1,0:T(1,128)} %bitcast.10, f32[1,1024]{1,0:T(1,128)} %bitcast.11, ...), custom_call_target="tpu_custom_call" | custom-call | flops 1800000000 | bytes 6291456 | tf_op jit(solution)/shard_map/pallas_call | solution.py:133
  20.5 8.6 %collective-permute-done = bf16[1024,128]{1,0:T(8,128)(2,1)S(1)} collective-permute-done((bf16[1024,128]{1,0:T(8,128)(2,1)S(1)}, bf16[1024,128]{1,0:T(8,128)(2,1)S(1)}, u32[]{:S(2)}, u32[]{:S(2)}) %collective-permute-start) | collective-permute-done | bytes 262176 | tf_op jit(solution)/shard_map/ppermute | solution.py:293
  29.1 2.0 %collective-permute-start.7 = (bf16[512,1024]{1,0:T(8,128)(2,1)}, bf16[512,1024]{1,0:T(8,128)(2,1)}, u32[]{:S(2)}, u32[]{:S(2)}) collective-permute-start(bf16[512,1024]{1,0:T(8,128)(2,1)} %shard_map.83.refs_0_), channel_id=1, source_target_pairs={{0,2},{1,35},{2,32},{3,1},{32,34},{33,3},{34,0},{35,33},{4,6},{5,3... | collective-permute-start | bytes 3145736 | tf_op jit(solution)/shard_map/ppermute | solution.py:287
  32.7 1.8 %collective-permute-start.5 = (bf16[1024,128]{1,0:T(8,128)(2,1)S(1)}, bf16[1024,128]{1,0:T(8,128)(2,1)S(1)}, u32[]{:S(2)}, u32[]{:S(2)}) collective-permute-start(bf16[1024,128]{1,0:T(8,128)(2,1)S(1)} %collective-permute-done), channel_id=1, source_target_pairs={{0,192},{64,0},{128,64},{192,128},{1,193},{65,1},{129,65},{193,129... | collective-permute-start | bytes 786440 | tf_op jit(solution)/shard_map/ppermute | solution.py:282
  34.4 3.8 %collective-permute-done.5.refs_9_ = bf16[1024,128]{1,0:T(8,128)(2,1)S(1)} collective-permute-done((bf16[1024,128]{1,0:T(8,128)(2,1)S(1)}, bf16[1024,128]{1,0:T(8,128)(2,1)S(1)}, u32[]{:S(2)}, u32[]{:S(2)}) %collective-permute-start.5) | collective-permute-done | bytes 262176 | tf_op jit(solution)/shard_map/ppermute | solution.py:282
  38.3 3.1 %collective-permute-done.6.refs_10_ = bf16[1024,128]{1,0:T(8,128)(2,1)S(1)} collective-permute-done((bf16[1024,128]{1,0:T(8,128)(2,1)S(1)}, bf16[1024,128]{1,0:T(8,128)(2,1)S(1)}, u32[]{:S(2)}, u32[]{:S(2)}) %collective-permute-start.6) | collective-permute-done | bytes 262176 | tf_op jit(solution)/shard_map/ppermute | solution.py:282
  41.7 2.1 %collective-permute-done.4.refs_14_ = bf16[2048,128]{1,0:T(8,128)(2,1)S(1)} collective-permute-done((bf16[2048,128]{1,0:T(8,128)(2,1)S(1)}, bf16[2048,128]{1,0:T(8,128)(2,1)S(1)}, u32[]{:S(2)}, u32[]{:S(2)}) %collective-permute-start.4) | collective-permute-done | bytes 524320 | tf_op jit(solution)/shard_map/ppermute | solution.py:282
  43.8 1.7 %collective-permute-done.7.refs_1_ = bf16[512,1024]{1,0:T(8,128)(2,1)} collective-permute-done((bf16[512,1024]{1,0:T(8,128)(2,1)}, bf16[512,1024]{1,0:T(8,128)(2,1)}, u32[]{:S(2)}, u32[]{:S(2)}) %collective-permute-start.7) | collective-permute-done | bytes 1048608 | tf_op jit(solution)/shard_map/ppermute | solution.py:287
  50.1 7.3 %collective-permute-done.10.refs_12_ = bf16[2048,128]{1,0:T(8,128)(2,1)S(1)} collective-permute-done((bf16[2048,128]{1,0:T(8,128)(2,1)S(1)}, bf16[2048,128]{1,0:T(8,128)(2,1)S(1)}, u32[]{:S(2)}, u32[]{:S(2)}) %collective-permute-start.10) | collective-permute-done | bytes 524320 | tf_op jit(solution)/shard_map/ppermute | solution.py:282
  60.9 1.9 %collective-permute-start.17 = (bf16[512,1024]{1,0:T(8,128)(2,1)}, bf16[512,1024]{1,0:T(8,128)(2,1)}, u32[]{:S(2)}, u32[]{:S(2)}) collective-permute-start(bf16[512,1024]{1,0:T(8,128)(2,1)} %collective-permute-done.7.refs_1_), channel_id=1, source_target_pairs={{0,2},{1,35},{2,32},{3,1},{32,34},{33,3},{34,0},{35,33},{4,6},{5,3... | collective-permute-start | bytes 3145736 | tf_op jit(solution)/shard_map/ppermute | solution.py:287
  62.8 1.9 %collective-permute-start.15 = (bf16[2048,128]{1,0:T(8,128)(2,1)S(1)}, bf16[2048,128]{1,0:T(8,128)(2,1)S(1)}, u32[]{:S(2)}, u32[]{:S(2)}) collective-permute-start(bf16[2048,128]{1,0:T(8,128)(2,1)S(1)} %pad_maximum_fusion.2), channel_id=1, source_target_pairs={{0,192},{64,0},{128,64},{192,128},{1,193},{65,1},{129,65},{193,129... | collective-permute-start | bytes 1572872 | tf_op jit(solution)/shard_map/ppermute | solution.py:282
  66.4 8.0 %collective-permute-done.15.refs_16_ = bf16[2048,128]{1,0:T(8,128)(2,1)S(1)} collective-permute-done((bf16[2048,128]{1,0:T(8,128)(2,1)S(1)}, bf16[2048,128]{1,0:T(8,128)(2,1)S(1)}, u32[]{:S(2)}, u32[]{:S(2)}) %collective-permute-start.15) | collective-permute-done | bytes 524320 | tf_op jit(solution)/shard_map/ppermute | solution.py:282
  75.9 2.6 %collective-permute-done.14.refs_4_ = bf16[2048,128]{1,0:T(8,128)(2,1)S(1)} collective-permute-done((bf16[2048,128]{1,0:T(8,128)(2,1)S(1)}, bf16[2048,128]{1,0:T(8,128)(2,1)S(1)}, u32[]{:S(2)}, u32[]{:S(2)}) %collective-permute-start.14) | collective-permute-done | bytes 524320 | tf_op jit(solution)/shard_map/ppermute | solution.py:282
  78.5 3.4 %collective-permute-start.21 = (bf16[512,1024]{1,0:T(8,128)(2,1)}, bf16[512,1024]{1,0:T(8,128)(2,1)}, u32[]{:S(2)}, u32[]{:S(2)}) collective-permute-start(bf16[512,1024]{1,0:T(8,128)(2,1)} %shard_map.83.refs_0_), channel_id=1, source_target_pairs={{0,1},{1,0},{2,3},{3,2},{4,5},{5,4},{6,7},{7,6},{8,9},{9,8},{10,11... | collective-permute-start | bytes 3145736 | tf_op jit(solution)/shard_map/ppermute | solution.py:297
  89.0 15.6 %shard_map.84 = (bf16[2,128,640]{2,1,0:T(8,128)(2,1)}, bf16[2,128,640]{2,1,0:T(8,128)(2,1)}, bf16[2,128,640]{2,1,0:T(8,128)(2,1)}, bf16[2,128,640]{2,1,0:T(8,128)(2,1)}, bf16[2,512,4096]{2,1,0:T(8,128)(2,1)S(1)}) custom-call(s32[4]{0:T(128)} %pad_add_fusion.where_ref, bf16[512,1024]{1,0:T(8,128)(2,1)} %shard_map.83.refs_0_, ...), custom_call_target="tpu_custom_call" | custom-call | flops 5368709120 | bytes 12582912 | tf_op jit(solution)/shard_map/pallas_call | solution.py:237
  106.3 2.5 %collective-permute-start.26 = (bf16[2,128,640]{2,1,0:T(8,128)(2,1)}, bf16[2,128,640]{2,1,0:T(8,128)(2,1)S(1)}, u32[]{:S(2)}, u32[]{:S(2)}) collective-permute-start(bf16[2,128,640]{2,1,0:T(8,128)(2,1)} %get-tuple-element.74), channel_id=1, source_target_pairs={{0,32},{2,34},{32,0},{34,2},{1,33},{3,35},{33,1},{35,3},{4,36},{6,... | collective-permute-start | bytes 983048 | tf_op jit(solution)/shard_map/ppermute | solution.py:282
  110.8 3.4 %shard_map.85.refs_4_ = bf16[8,128,256]{2,1,0:T(8,128)(2,1)S(1)} custom-call(s32[4]{0:T(128)S(1)} %copy-done.1, bf16[2,512,4096]{2,1,0:T(8,128)(2,1)S(1)} %get-tuple-element.76.refs_0_, bf16[2048,128]{1,0:T(8,128)(2,1)S(1)} %collective-permute-done.13.refs_1_, bf16[2048,128]{1,0:T(8,128)(2,1)S(1)} %collective-permute-done.19.refs_2_, ...), custom_call_target="tpu_custom_call" | custom-call | flops 2147483648 | bytes 12582912 | tf_op jit(solution)/shard_map/pallas_call | solution.py:237
  115.2 3.9 %shard_map.86 = bf16[8,128,384]{2,1,0:T(8,128)(2,1)} custom-call(s32[4]{0:T(128)S(1)} %copy-done.1, bf16[2,512,4096]{2,1,0:T(8,128)(2,1)S(1)} %get-tuple-element.76.refs_0_, bf16[2048,128]{1,0:T(8,128)(2,1)S(1)} %collective-permute-done.18.refs_1_, bf16[1024,128]{1,0:T(8,128)(2,1)S(1)} %collective-permute-done.29.refs_2_, ...), custom_call_target="tpu_custom_call" | custom-call | flops 1073741824 | bytes 12582912 | tf_op jit(solution)/shard_map/pallas_call | solution.py:237
  119.1 4.7 %all-to-all-start = ((bf16[8,128,384]{2,1,0:T(8,128)(2,1)}), bf16[8,128,384]{2,1,0:T(8,128)(2,1)S(1)}, u32[]{:S(2)}, u32[]{:S(2)}) async-start(bf16[8,128,384]{2,1,0:T(8,128)(2,1)} %shard_map.86), calls=%async_computation | async-start | bytes 1572864 | tf_op jit(solution)/shard_map/all_to_all | solution.py:380
  126.5 9.6 %all-to-all-done.refs_5_ = bf16[8,128,384]{2,1,0:T(8,128)(2,1)S(1)} async-done(((bf16[8,128,384]{2,1,0:T(8,128)(2,1)}), bf16[8,128,384]{2,1,0:T(8,128)(2,1)S(1)}, u32[]{:S(2)}, u32[]{:S(2)}) %all-to-all-start) | async-done | bytes 786464 | tf_op jit(solution)/shard_map/all_to_all | solution.py:380
  136.1 2.3 %shard_map.87 = bf16[128,8192]{1,0:T(8,128)(2,1)} custom-call(s32[4]{0:T(128)S(1)} %copy-done.1, bf16[2,128,640]{2,1,0:T(8,128)(2,1)S(1)} %copy-done, bf16[2,128,640]{2,1,0:T(8,128)(2,1)S(1)} %collective-permute-done.25.refs_1_, bf16[2,128,640]{2,1,0:T(8,128)(2,1)S(1)} %collective-permute-done.26.refs_2_, ...), custom_call_target="tpu_custom_call" | custom-call | bytes 4194304 | tf_op jit(solution)/shard_map/pallas_call | solution.py:270
  (94 shorter events, 28.4 us)
Async XLA Ops:
  2.2 10.3 %collective-permute-start.2 = (bf16[144,1024]{1,0:T(8,128)(2,1)}, bf16[144,1024]{1,0:T(8,128)(2,1)S(1)}, u32[]{:S(2)}, u32[]{:S(2)}) collective-permute-start(bf16[144,1024]{1,0:T(8,128)(2,1)} %shard_map.82), channel_id=1, source_target_pairs={{0,4},{4,8},{8,12},{12,16},{16,20},{20,24},{24,28},{28,32},{32,36}... | collective-permute-start | bytes 884744 | tf_op jit(solution)/shard_map/ppermute | solution.py:348
  6.6 22.5 %collective-permute-start = (bf16[1024,128]{1,0:T(8,128)(2,1)S(1)}, bf16[1024,128]{1,0:T(8,128)(2,1)S(1)}, u32[]{:S(2)}, u32[]{:S(2)}) collective-permute-start(bf16[1024,128]{1,0:T(8,128)(2,1)S(1)} %copy-done.12), channel_id=1, source_target_pairs={{0,0},{1,128},{2,64},{3,192},{64,1},{65,129},{66,65},{67,193},{128... | collective-permute-start | bytes 786440 | tf_op jit(solution)/shard_map/ppermute | solution.py:293
  12.2 16.8 %collective-permute-start.1 = (bf16[1024,128]{1,0:T(8,128)(2,1)S(1)}, bf16[1024,128]{1,0:T(8,128)(2,1)S(1)}, u32[]{:S(2)}, u32[]{:S(2)}) collective-permute-start(bf16[1024,128]{1,0:T(8,128)(2,1)S(1)} %copy-done.12), channel_id=1, source_target_pairs={{0,128},{1,0},{2,192},{3,64},{64,129},{65,1},{66,193},{67,65},{128... | collective-permute-start | bytes 786440 | tf_op jit(solution)/shard_map/ppermute | solution.py:293
  29.1 16.4 %collective-permute-start.7 = (bf16[512,1024]{1,0:T(8,128)(2,1)}, bf16[512,1024]{1,0:T(8,128)(2,1)}, u32[]{:S(2)}, u32[]{:S(2)}) collective-permute-start(bf16[512,1024]{1,0:T(8,128)(2,1)} %shard_map.83.refs_0_), channel_id=1, source_target_pairs={{0,2},{1,35},{2,32},{3,1},{32,34},{33,3},{34,0},{35,33},{4,6},{5,3... | collective-permute-start | bytes 3145736 | tf_op jit(solution)/shard_map/ppermute | solution.py:287
  31.1 10.6 %collective-permute-start.3 = (bf16[2048,128]{1,0:T(8,128)(2,1)S(1)}, bf16[2048,128]{1,0:T(8,128)(2,1)S(1)}, u32[]{:S(2)}, u32[]{:S(2)}) collective-permute-start(bf16[2048,128]{1,0:T(8,128)(2,1)S(1)} %constant_dynamic-update-slice_fusion.refs_8_), channel_id=1, source_target_pairs={{0,28},{4,0},{8,4},{12,8},{16,12},{20,16},{24,20},{28,24},{1,29},{... | collective-permute-start | bytes 1572872 | tf_op jit(solution)/shard_map/ppermute | solution.py:282
  31.7 12.1 %collective-permute-start.4 = (bf16[2048,128]{1,0:T(8,128)(2,1)S(1)}, bf16[2048,128]{1,0:T(8,128)(2,1)S(1)}, u32[]{:S(2)}, u32[]{:S(2)}) collective-permute-start(bf16[2048,128]{1,0:T(8,128)(2,1)S(1)} %constant_dynamic-update-slice_fusion.refs_8_), channel_id=1, source_target_pairs={{0,4},{4,8},{8,12},{12,16},{16,20},{20,24},{24,28},{28,0},{1,5},{5... | collective-permute-start | bytes 1572872 | tf_op jit(solution)/shard_map/ppermute | solution.py:282
  45.5 15.4 %collective-permute-start.12 = (bf16[512,1024]{1,0:T(8,128)(2,1)}, bf16[512,1024]{1,0:T(8,128)(2,1)}, u32[]{:S(2)}, u32[]{:S(2)}) collective-permute-start(bf16[512,1024]{1,0:T(8,128)(2,1)} %shard_map.83.refs_0_), channel_id=1, source_target_pairs={{0,34},{1,3},{2,0},{3,33},{32,2},{33,35},{34,32},{35,1},{4,38},{5,... | collective-permute-start | bytes 3145736 | tf_op jit(solution)/shard_map/ppermute | solution.py:287
  47.0 10.4 %collective-permute-start.10 = (bf16[2048,128]{1,0:T(8,128)(2,1)S(1)}, bf16[2048,128]{1,0:T(8,128)(2,1)S(1)}, u32[]{:S(2)}, u32[]{:S(2)}) collective-permute-start(bf16[2048,128]{1,0:T(8,128)(2,1)S(1)} %pad_maximum_fusion.1), channel_id=1, source_target_pairs={{0,192},{64,0},{128,64},{192,128},{1,193},{65,1},{129,65},{193,129... | collective-permute-start | bytes 1572872 | tf_op jit(solution)/shard_map/ppermute | solution.py:282
  47.9 10.5 %collective-permute-start.11 = (bf16[2048,128]{1,0:T(8,128)(2,1)S(1)}, bf16[2048,128]{1,0:T(8,128)(2,1)S(1)}, u32[]{:S(2)}, u32[]{:S(2)}) collective-permute-start(bf16[2048,128]{1,0:T(8,128)(2,1)S(1)} %pad_maximum_fusion.1), channel_id=1, source_target_pairs={{0,64},{64,128},{128,192},{192,0},{1,65},{65,129},{129,193},{193,1... | collective-permute-start | bytes 1572872 | tf_op jit(solution)/shard_map/ppermute | solution.py:282
  48.6 9.8 %collective-permute-start.8 = (bf16[2048,128]{1,0:T(8,128)(2,1)S(1)}, bf16[2048,128]{1,0:T(8,128)(2,1)S(1)}, u32[]{:S(2)}, u32[]{:S(2)}) collective-permute-start(bf16[2048,128]{1,0:T(8,128)(2,1)S(1)} %collective-permute-done.3.refs_11_), channel_id=1, source_target_pairs={{0,28},{4,0},{8,4},{12,8},{16,12},{20,16},{24,20},{28,24},{1,29},{... | collective-permute-start | bytes 1572872 | tf_op jit(solution)/shard_map/ppermute | solution.py:282
  48.6 10.8 %collective-permute-start.9 = (bf16[2048,128]{1,0:T(8,128)(2,1)S(1)}, bf16[2048,128]{1,0:T(8,128)(2,1)S(1)}, u32[]{:S(2)}, u32[]{:S(2)}) collective-permute-start(bf16[2048,128]{1,0:T(8,128)(2,1)S(1)} %collective-permute-done.4.refs_14_), channel_id=1, source_target_pairs={{0,4},{4,8},{8,12},{12,16},{16,20},{20,24},{24,28},{28,0},{1,5},{5... | collective-permute-start | bytes 1572872 | tf_op jit(solution)/shard_map/ppermute | solution.py:282
  60.9 17.7 %collective-permute-start.17 = (bf16[512,1024]{1,0:T(8,128)(2,1)}, bf16[512,1024]{1,0:T(8,128)(2,1)}, u32[]{:S(2)}, u32[]{:S(2)}) collective-permute-start(bf16[512,1024]{1,0:T(8,128)(2,1)} %collective-permute-done.7.refs_1_), channel_id=1, source_target_pairs={{0,2},{1,35},{2,32},{3,1},{32,34},{33,3},{34,0},{35,33},{4,6},{5,3... | collective-permute-start | bytes 3145736 | tf_op jit(solution)/shard_map/ppermute | solution.py:287
  62.8 11.6 %collective-permute-start.15 = (bf16[2048,128]{1,0:T(8,128)(2,1)S(1)}, bf16[2048,128]{1,0:T(8,128)(2,1)S(1)}, u32[]{:S(2)}, u32[]{:S(2)}) collective-permute-start(bf16[2048,128]{1,0:T(8,128)(2,1)S(1)} %pad_maximum_fusion.2), channel_id=1, source_target_pairs={{0,192},{64,0},{128,64},{192,128},{1,193},{65,1},{129,65},{193,129... | collective-permute-start | bytes 1572872 | tf_op jit(solution)/shard_map/ppermute | solution.py:282
  64.8 11.1 %collective-permute-start.16 = (bf16[2048,128]{1,0:T(8,128)(2,1)S(1)}, bf16[2048,128]{1,0:T(8,128)(2,1)S(1)}, u32[]{:S(2)}, u32[]{:S(2)}) collective-permute-start(bf16[2048,128]{1,0:T(8,128)(2,1)S(1)} %pad_maximum_fusion.2), channel_id=1, source_target_pairs={{0,64},{64,128},{128,192},{192,0},{1,65},{65,129},{129,193},{193,1... | collective-permute-start | bytes 1572872 | tf_op jit(solution)/shard_map/ppermute | solution.py:282
  64.9 11.0 %collective-permute-start.13 = (bf16[2048,128]{1,0:T(8,128)(2,1)S(1)}, bf16[2048,128]{1,0:T(8,128)(2,1)S(1)}, u32[]{:S(2)}, u32[]{:S(2)}) collective-permute-start(bf16[2048,128]{1,0:T(8,128)(2,1)S(1)} %collective-permute-done.8.refs_15_), channel_id=1, source_target_pairs={{0,28},{4,0},{8,4},{12,8},{16,12},{20,16},{24,20},{28,24},{1,29},{... | collective-permute-start | bytes 1572872 | tf_op jit(solution)/shard_map/ppermute | solution.py:282
  65.3 13.2 %collective-permute-start.14 = (bf16[2048,128]{1,0:T(8,128)(2,1)S(1)}, bf16[2048,128]{1,0:T(8,128)(2,1)S(1)}, u32[]{:S(2)}, u32[]{:S(2)}) collective-permute-start(bf16[2048,128]{1,0:T(8,128)(2,1)S(1)} %collective-permute-done.9.refs_18_), channel_id=1, source_target_pairs={{0,4},{4,8},{8,12},{12,16},{16,20},{20,24},{24,28},{28,0},{1,5},{5... | collective-permute-start | bytes 1572872 | tf_op jit(solution)/shard_map/ppermute | solution.py:282
  82.7 22.0 %collective-permute-start.19 = (bf16[2048,128]{1,0:T(8,128)(2,1)S(1)}, bf16[2048,128]{1,0:T(8,128)(2,1)S(1)}, u32[]{:S(2)}, u32[]{:S(2)}) collective-permute-start(bf16[2048,128]{1,0:T(8,128)(2,1)S(1)} %pad_maximum_fusion.3), channel_id=1, source_target_pairs={{0,192},{64,0},{128,64},{192,128},{1,193},{65,1},{129,65},{193,129... | collective-permute-start | bytes 1572872 | tf_op jit(solution)/shard_map/ppermute | solution.py:282
  84.5 20.1 %collective-permute-start.20 = (bf16[2048,128]{1,0:T(8,128)(2,1)S(1)}, bf16[2048,128]{1,0:T(8,128)(2,1)S(1)}, u32[]{:S(2)}, u32[]{:S(2)}) collective-permute-start(bf16[2048,128]{1,0:T(8,128)(2,1)S(1)} %pad_maximum_fusion.3), channel_id=1, source_target_pairs={{0,64},{64,128},{128,192},{192,0},{1,65},{65,129},{129,193},{193,1... | collective-permute-start | bytes 1572872 | tf_op jit(solution)/shard_map/ppermute | solution.py:282
  86.0 18.6 %collective-permute-start.18 = (bf16[2048,128]{1,0:T(8,128)(2,1)S(1)}, bf16[2048,128]{1,0:T(8,128)(2,1)S(1)}, u32[]{:S(2)}, u32[]{:S(2)}) collective-permute-start(bf16[2048,128]{1,0:T(8,128)(2,1)S(1)} %collective-permute-done.13.refs_1_), channel_id=1, source_target_pairs={{0,28},{4,0},{8,4},{12,8},{16,12},{20,16},{24,20},{28,24},{1,29},{... | collective-permute-start | bytes 1572872 | tf_op jit(solution)/shard_map/ppermute | solution.py:282
  106.3 17.5 %collective-permute-start.25 = (bf16[2,128,640]{2,1,0:T(8,128)(2,1)}, bf16[2,128,640]{2,1,0:T(8,128)(2,1)S(1)}, u32[]{:S(2)}, u32[]{:S(2)}) collective-permute-start(bf16[2,128,640]{2,1,0:T(8,128)(2,1)} %get-tuple-element.73), channel_id=1, source_target_pairs={{0,2},{2,32},{32,34},{34,0},{1,3},{3,33},{33,35},{35,1},{4,6},{6,3... | collective-permute-start | bytes 983048 | tf_op jit(solution)/shard_map/ppermute | solution.py:282
  106.3 17.5 %collective-permute-start.26 = (bf16[2,128,640]{2,1,0:T(8,128)(2,1)}, bf16[2,128,640]{2,1,0:T(8,128)(2,1)S(1)}, u32[]{:S(2)}, u32[]{:S(2)}) collective-permute-start(bf16[2,128,640]{2,1,0:T(8,128)(2,1)} %get-tuple-element.74), channel_id=1, source_target_pairs={{0,32},{2,34},{32,0},{34,2},{1,33},{3,35},{33,1},{35,3},{4,36},{6,... | collective-permute-start | bytes 983048 | tf_op jit(solution)/shard_map/ppermute | solution.py:282
  108.8 15.2 %collective-permute-start.27 = (bf16[2,128,640]{2,1,0:T(8,128)(2,1)}, bf16[2,128,640]{2,1,0:T(8,128)(2,1)S(1)}, u32[]{:S(2)}, u32[]{:S(2)}) collective-permute-start(bf16[2,128,640]{2,1,0:T(8,128)(2,1)} %get-tuple-element.75), channel_id=1, source_target_pairs={{0,34},{2,0},{32,2},{34,32},{1,35},{3,1},{33,3},{35,33},{4,38},{6,... | collective-permute-start | bytes 983048 | tf_op jit(solution)/shard_map/ppermute | solution.py:282
  119.1 17.0 %all-to-all-start = ((bf16[8,128,384]{2,1,0:T(8,128)(2,1)}), bf16[8,128,384]{2,1,0:T(8,128)(2,1)S(1)}, u32[]{:S(2)}, u32[]{:S(2)}) async-start(bf16[8,128,384]{2,1,0:T(8,128)(2,1)} %shard_map.86), calls=%async_computation | async-start | bytes 1572864 | tf_op jit(solution)/shard_map/all_to_all | solution.py:380
  125.0 11.1 %collective-permute-start.28 = (bf16[4,128,640]{2,1,0:T(8,128)(2,1)}, bf16[4,128,640]{2,1,0:T(8,128)(2,1)S(1)}, u32[]{:S(2)}, u32[]{:S(2)}) collective-permute-start(bf16[4,128,640]{2,1,0:T(8,128)(2,1)} %pad_maximum_fusion), channel_id=1, source_target_pairs={{0,1},{1,0},{2,3},{3,2},{4,5},{5,4},{6,7},{7,6},{8,9},{9,8},{10,11... | collective-permute-start | bytes 1966088 | tf_op jit(solution)/shard_map/ppermute | solution.py:297
  (23 other events, 385.4 us)

commit v4 on v3

--- a/solution.py
+++ b/solution.py
@@ -185,10 +185,12 @@
         start = pl.multiple_of(k_block(y, kind) * CH, CH)
         target = weight.at[pl.ds(start, CH), pl.ds(col * 128, 128)]
         copies.append(pltpu.make_async_copy(src[piece].at[pl.ds(row, CH)], target, sems.at[n]))
-    for copy in act_copies[:1] + act_copies[4:5] + copies + act_copies[1:4] + act_copies[5:]:
+    ahead = [[], [], []]
+    for copy, (piece, row, col, kind) in zip(copies, moves, strict=True):
+        ahead[col // 2].append(copy)
+    order = act_copies[0:1] + act_copies[4:5] + ahead[0] + act_copies[1:3] + act_copies[5:7] + ahead[1] + ahead[2]
+    for copy in order + act_copies[3:4] + act_copies[7:8]:
         copy.start()
-    for copy in copies:
-        copy.wait()
     columns = weight.shape[1]
     for turn in range(2):
         half = x // 2 if turn == 0 else 1 - x // 2
@@ -196,7 +198,10 @@
             view = acts.at[half, :, pl.ds(block * CH, CH)]
             pltpu.make_async_copy(act_refs[0], view, act_sems.at[half, block]).wait()
         rows = pl.ds(pl.multiple_of(half * TOK, TOK), TOK)
-        for at in range(0, columns, 256):
+        for p, at in enumerate(range(0, columns, 256)):
+            if turn == 0:
+                for copy in ahead[p]:
+                    copy.wait()
             span = slice(at, min(at + 256, columns))
             result[rows, span] = jnp.dot(acts[half], weight[:, span], preferred_element_type=F32).astype(BF16)
     if absolute:

time: 139 us -> 141 us (1.014)
  Pallas kernels: 34.7 us -> 36.8 us
    pallas_call x3, Pallas kernels: 22.9 us -> 25.1 us  [project(): pl.pallas_call(functools.partial(project_kernel, len(pieces), moves, abso...]
  transfers between devices with their start and end apart: 32 -> 32, of which waited for: 20 -> 20; matrix products, arithmetic and copies ran while one was open for 2% -> 2% of each run, Pallas kernels for 22% -> 23%
where the time goes in v4:
time: 141 us
  waiting for transfers between devices  56.2 us (40%)
  starting transfers between devices  43.7 us (31%)
  Pallas kernels  36.8 us (26%)
  local copies, waits for them, and re-layouts  1.92 us (1%)
  other arithmetic  1.73 us (1%)
    ppermute x20, waiting for transfers between devices, shift(): lax.ppermute(value, axis, [(i, (i + steps) % size) for i in range(size)])  32.2 us
    pallas_call x3, Pallas kernels, project(): pl.pallas_call(functools.partial(project_kernel, len(pieces), moves, abso...  25.1 us
    ppermute x20, starting transfers between devices, shift(): lax.ppermute(value, axis, [(i, (i + steps) % size) for i in range(size)])  18.2 us
    all_to_all x1, waiting for transfers between devices, on_device(): last_got = lax.all_to_all(last_sent, RING + ('c',), 0, 0, tiled=True)  9.64 us
    ppermute x2, waiting for transfers between devices, exchange(): return lax.ppermute(value, ('y', 'xl', 'c'), pairs)  8.58 us
    pallas_call x1, Pallas kernels, mixer(): pl.pallas_call(mixer_kernel, grid=(steps,), in_specs=[pl.BlockSpec((3, TO...  7.23 us
    ppermute x2, starting transfers between devices, exchange(): return lax.ppermute(value, ('y', 'xl', 'c'), pairs)  5.74 us
    ppermute x5, starting transfers between devices, swap_cores(): return lax.ppermute(value, 'c', [(0, 1), (1, 0)])  5.43 us
  transfers between devices with their start and end apart: 32, of which 20 were waited for; matrix products, arithmetic and copies ran while one was open for 2% of the time, Pallas kernels for 23%

profile of v4, /device:TPU:1, one launch (start us, length us, event | category | flops | bytes accessed | tf_op | source)
XLA Modules:
  0.0 140.6 jit_solution(4674000255538803083)
XLA Ops:
  0.0 2.2 %shard_map.82 = bf16[144,1024]{1,0:T(8,128)(2,1)} custom-call(bf16[3,512,1024]{2,1,0:T(8,128)(2,1)} %bitcast.7, bf16[3,512,1024]{2,1,0:T(8,128)(2,1)} %bitcast.8, f32[3,3,1024]{2,1,0:T(4,128)} %taps_ref.3), custom_call_target="tpu_custom_call" | custom-call | flops 524288 | bytes 2097152 | tf_op jit(solution)/shard_map/pallas_call | solution.py:74
  2.2 4.4 %collective-permute-start.2 = (bf16[144,1024]{1,0:T(8,128)(2,1)}, bf16[144,1024]{1,0:T(8,128)(2,1)S(1)}, u32[]{:S(2)}, u32[]{:S(2)}) collective-permute-start(bf16[144,1024]{1,0:T(8,128)(2,1)} %shard_map.82), channel_id=1, source_target_pairs={{0,4},{4,8},{8,12},{12,16},{16,20},{20,24},{24,28},{28,32},{32,36}... | collective-permute-start | bytes 884744 | tf_op jit(solution)/shard_map/ppermute | solution.py:353
  6.6 5.6 %collective-permute-start = (bf16[1024,128]{1,0:T(8,128)(2,1)S(1)}, bf16[1024,128]{1,0:T(8,128)(2,1)S(1)}, u32[]{:S(2)}, u32[]{:S(2)}) collective-permute-start(bf16[1024,128]{1,0:T(8,128)(2,1)S(1)} %copy-done.12), channel_id=1, source_target_pairs={{0,0},{1,128},{2,64},{3,192},{64,1},{65,129},{66,65},{67,193},{128... | collective-permute-start | bytes 786440 | tf_op jit(solution)/shard_map/ppermute | solution.py:298
  13.2 7.2 %shard_map.83.refs_0_ = bf16[512,1024]{1,0:T(8,128)(2,1)} custom-call(bf16[3,512,1024]{2,1,0:T(8,128)(2,1)} %bitcast.9, bf16[144,1024]{1,0:T(8,128)(2,1)} %copy-done.11, f32[3,3,1024]{2,1,0:T(4,128)} %taps_ref.3, f32[1024,128]{1,0:T(8,128)} %filt_ref.1, f32[1,1024]{1,0:T(1,128)} %bitcast.10, f32[1,1024]{1,0:T(1,128)} %bitcast.11, ...), custom_call_target="tpu_custom_call" | custom-call | flops 1800000000 | bytes 6291456 | tf_op jit(solution)/shard_map/pallas_call | solution.py:133
  20.5 8.6 %collective-permute-done = bf16[1024,128]{1,0:T(8,128)(2,1)S(1)} collective-permute-done((bf16[1024,128]{1,0:T(8,128)(2,1)S(1)}, bf16[1024,128]{1,0:T(8,128)(2,1)S(1)}, u32[]{:S(2)}, u32[]{:S(2)}) %collective-permute-start) | collective-permute-done | bytes 262176 | tf_op jit(solution)/shard_map/ppermute | solution.py:298
  29.1 2.0 %collective-permute-start.7 = (bf16[512,1024]{1,0:T(8,128)(2,1)}, bf16[512,1024]{1,0:T(8,128)(2,1)}, u32[]{:S(2)}, u32[]{:S(2)}) collective-permute-start(bf16[512,1024]{1,0:T(8,128)(2,1)} %shard_map.83.refs_0_), channel_id=1, source_target_pairs={{0,2},{1,35},{2,32},{3,1},{32,34},{33,3},{34,0},{35,33},{4,6},{5,3... | collective-permute-start | bytes 3145736 | tf_op jit(solution)/shard_map/ppermute | solution.py:292
  32.7 1.8 %collective-permute-start.5 = (bf16[1024,128]{1,0:T(8,128)(2,1)S(1)}, bf16[1024,128]{1,0:T(8,128)(2,1)S(1)}, u32[]{:S(2)}, u32[]{:S(2)}) collective-permute-start(bf16[1024,128]{1,0:T(8,128)(2,1)S(1)} %collective-permute-done), channel_id=1, source_target_pairs={{0,192},{64,0},{128,64},{192,128},{1,193},{65,1},{129,65},{193,129... | collective-permute-start | bytes 786440 | tf_op jit(solution)/shard_map/ppermute | solution.py:287
  34.4 3.8 %collective-permute-done.5.refs_9_ = bf16[1024,128]{1,0:T(8,128)(2,1)S(1)} collective-permute-done((bf16[1024,128]{1,0:T(8,128)(2,1)S(1)}, bf16[1024,128]{1,0:T(8,128)(2,1)S(1)}, u32[]{:S(2)}, u32[]{:S(2)}) %collective-permute-start.5) | collective-permute-done | bytes 262176 | tf_op jit(solution)/shard_map/ppermute | solution.py:287
  38.3 3.1 %collective-permute-done.6.refs_10_ = bf16[1024,128]{1,0:T(8,128)(2,1)S(1)} collective-permute-done((bf16[1024,128]{1,0:T(8,128)(2,1)S(1)}, bf16[1024,128]{1,0:T(8,128)(2,1)S(1)}, u32[]{:S(2)}, u32[]{:S(2)}) %collective-permute-start.6) | collective-permute-done | bytes 262176 | tf_op jit(solution)/shard_map/ppermute | solution.py:287
  41.7 2.1 %collective-permute-done.4.refs_14_ = bf16[2048,128]{1,0:T(8,128)(2,1)S(1)} collective-permute-done((bf16[2048,128]{1,0:T(8,128)(2,1)S(1)}, bf16[2048,128]{1,0:T(8,128)(2,1)S(1)}, u32[]{:S(2)}, u32[]{:S(2)}) %collective-permute-start.4) | collective-permute-done | bytes 524320 | tf_op jit(solution)/shard_map/ppermute | solution.py:287
  43.8 1.7 %collective-permute-done.7.refs_1_ = bf16[512,1024]{1,0:T(8,128)(2,1)} collective-permute-done((bf16[512,1024]{1,0:T(8,128)(2,1)}, bf16[512,1024]{1,0:T(8,128)(2,1)}, u32[]{:S(2)}, u32[]{:S(2)}) %collective-permute-start.7) | collective-permute-done | bytes 1048608 | tf_op jit(solution)/shard_map/ppermute | solution.py:292
  50.1 7.3 %collective-permute-done.10.refs_12_ = bf16[2048,128]{1,0:T(8,128)(2,1)S(1)} collective-permute-done((bf16[2048,128]{1,0:T(8,128)(2,1)S(1)}, bf16[2048,128]{1,0:T(8,128)(2,1)S(1)}, u32[]{:S(2)}, u32[]{:S(2)}) %collective-permute-start.10) | collective-permute-done | bytes 524320 | tf_op jit(solution)/shard_map/ppermute | solution.py:287
  60.9 1.9 %collective-permute-start.17 = (bf16[512,1024]{1,0:T(8,128)(2,1)}, bf16[512,1024]{1,0:T(8,128)(2,1)}, u32[]{:S(2)}, u32[]{:S(2)}) collective-permute-start(bf16[512,1024]{1,0:T(8,128)(2,1)} %collective-permute-done.7.refs_1_), channel_id=1, source_target_pairs={{0,2},{1,35},{2,32},{3,1},{32,34},{33,3},{34,0},{35,33},{4,6},{5,3... | collective-permute-start | bytes 3145736 | tf_op jit(solution)/shard_map/ppermute | solution.py:292
  62.8 1.9 %collective-permute-start.15 = (bf16[2048,128]{1,0:T(8,128)(2,1)S(1)}, bf16[2048,128]{1,0:T(8,128)(2,1)S(1)}, u32[]{:S(2)}, u32[]{:S(2)}) collective-permute-start(bf16[2048,128]{1,0:T(8,128)(2,1)S(1)} %pad_maximum_fusion.2), channel_id=1, source_target_pairs={{0,192},{64,0},{128,64},{192,128},{1,193},{65,1},{129,65},{193,129... | collective-permute-start | bytes 1572872 | tf_op jit(solution)/shard_map/ppermute | solution.py:287
  66.4 8.0 %collective-permute-done.15.refs_16_ = bf16[2048,128]{1,0:T(8,128)(2,1)S(1)} collective-permute-done((bf16[2048,128]{1,0:T(8,128)(2,1)S(1)}, bf16[2048,128]{1,0:T(8,128)(2,1)S(1)}, u32[]{:S(2)}, u32[]{:S(2)}) %collective-permute-start.15) | collective-permute-done | bytes 524320 | tf_op jit(solution)/shard_map/ppermute | solution.py:287
  75.9 2.6 %collective-permute-done.14.refs_4_ = bf16[2048,128]{1,0:T(8,128)(2,1)S(1)} collective-permute-done((bf16[2048,128]{1,0:T(8,128)(2,1)S(1)}, bf16[2048,128]{1,0:T(8,128)(2,1)S(1)}, u32[]{:S(2)}, u32[]{:S(2)}) %collective-permute-start.14) | collective-permute-done | bytes 524320 | tf_op jit(solution)/shard_map/ppermute | solution.py:287
  78.5 3.4 %collective-permute-start.21 = (bf16[512,1024]{1,0:T(8,128)(2,1)}, bf16[512,1024]{1,0:T(8,128)(2,1)}, u32[]{:S(2)}, u32[]{:S(2)}) collective-permute-start(bf16[512,1024]{1,0:T(8,128)(2,1)} %shard_map.83.refs_0_), channel_id=1, source_target_pairs={{0,1},{1,0},{2,3},{3,2},{4,5},{5,4},{6,7},{7,6},{8,9},{9,8},{10,11... | collective-permute-start | bytes 3145736 | tf_op jit(solution)/shard_map/ppermute | solution.py:302
  89.0 17.7 %shard_map.84 = (bf16[2,128,640]{2,1,0:T(8,128)(2,1)}, bf16[2,128,640]{2,1,0:T(8,128)(2,1)}, bf16[2,128,640]{2,1,0:T(8,128)(2,1)}, bf16[2,128,640]{2,1,0:T(8,128)(2,1)}, bf16[2,512,4096]{2,1,0:T(8,128)(2,1)S(1)}) custom-call(s32[4]{0:T(128)} %pad_add_fusion.where_ref, bf16[512,1024]{1,0:T(8,128)(2,1)} %shard_map.83.refs_0_, ...), custom_call_target="tpu_custom_call" | custom-call | flops 5368709120 | bytes 12582912 | tf_op jit(solution)/shard_map/pallas_call | solution.py:242
  108.4 2.3 %collective-permute-start.26 = (bf16[2,128,640]{2,1,0:T(8,128)(2,1)}, bf16[2,128,640]{2,1,0:T(8,128)(2,1)S(1)}, u32[]{:S(2)}, u32[]{:S(2)}) collective-permute-start(bf16[2,128,640]{2,1,0:T(8,128)(2,1)} %get-tuple-element.74), channel_id=1, source_target_pairs={{0,32},{2,34},{32,0},{34,2},{1,33},{3,35},{33,1},{35,3},{4,36},{6,... | collective-permute-start | bytes 983048 | tf_op jit(solution)/shard_map/ppermute | solution.py:287
  112.9 3.4 %shard_map.85.refs_4_ = bf16[8,128,256]{2,1,0:T(8,128)(2,1)S(1)} custom-call(s32[4]{0:T(128)S(1)} %copy-done.1, bf16[2,512,4096]{2,1,0:T(8,128)(2,1)S(1)} %get-tuple-element.76.refs_0_, bf16[2048,128]{1,0:T(8,128)(2,1)S(1)} %collective-permute-done.13.refs_1_, bf16[2048,128]{1,0:T(8,128)(2,1)S(1)} %collective-permute-done.19.refs_2_, ...), custom_call_target="tpu_custom_call" | custom-call | flops 2147483648 | bytes 12582912 | tf_op jit(solution)/shard_map/pallas_call | solution.py:242
  117.4 3.9 %shard_map.86 = bf16[8,128,384]{2,1,0:T(8,128)(2,1)} custom-call(s32[4]{0:T(128)S(1)} %copy-done.1, bf16[2,512,4096]{2,1,0:T(8,128)(2,1)S(1)} %get-tuple-element.76.refs_0_, bf16[2048,128]{1,0:T(8,128)(2,1)S(1)} %collective-permute-done.18.refs_1_, bf16[1024,128]{1,0:T(8,128)(2,1)S(1)} %collective-permute-done.29.refs_2_, ...), custom_call_target="tpu_custom_call" | custom-call | flops 1073741824 | bytes 12582912 | tf_op jit(solution)/shard_map/pallas_call | solution.py:242
  121.4 4.5 %all-to-all-start = ((bf16[8,128,384]{2,1,0:T(8,128)(2,1)}), bf16[8,128,384]{2,1,0:T(8,128)(2,1)S(1)}, u32[]{:S(2)}, u32[]{:S(2)}) async-start(bf16[8,128,384]{2,1,0:T(8,128)(2,1)} %shard_map.86), calls=%async_computation | async-start | bytes 1572864 | tf_op jit(solution)/shard_map/all_to_all | solution.py:385
  128.6 9.6 %all-to-all-done.refs_5_ = bf16[8,128,384]{2,1,0:T(8,128)(2,1)S(1)} async-done(((bf16[8,128,384]{2,1,0:T(8,128)(2,1)}), bf16[8,128,384]{2,1,0:T(8,128)(2,1)S(1)}, u32[]{:S(2)}, u32[]{:S(2)}) %all-to-all-start) | async-done | bytes 786464 | tf_op jit(solution)/shard_map/all_to_all | solution.py:385
  138.2 2.3 %shard_map.87 = bf16[128,8192]{1,0:T(8,128)(2,1)} custom-call(s32[4]{0:T(128)S(1)} %copy-done.1, bf16[2,128,640]{2,1,0:T(8,128)(2,1)S(1)} %copy-done, bf16[2,128,640]{2,1,0:T(8,128)(2,1)S(1)} %collective-permute-done.25.refs_1_, bf16[2,128,640]{2,1,0:T(8,128)(2,1)S(1)} %collective-permute-done.26.refs_2_, ...), custom_call_target="tpu_custom_call" | custom-call | bytes 4194304 | tf_op jit(solution)/shard_map/pallas_call | solution.py:275
  (94 shorter events, 28.7 us)
Async XLA Ops:
  2.2 10.3 %collective-permute-start.2 = (bf16[144,1024]{1,0:T(8,128)(2,1)}, bf16[144,1024]{1,0:T(8,128)(2,1)S(1)}, u32[]{:S(2)}, u32[]{:S(2)}) collective-permute-start(bf16[144,1024]{1,0:T(8,128)(2,1)} %shard_map.82), channel_id=1, source_target_pairs={{0,4},{4,8},{8,12},{12,16},{16,20},{20,24},{24,28},{28,32},{32,36}... | collective-permute-start | bytes 884744 | tf_op jit(solution)/shard_map/ppermute | solution.py:353
  6.6 22.5 %collective-permute-start = (bf16[1024,128]{1,0:T(8,128)(2,1)S(1)}, bf16[1024,128]{1,0:T(8,128)(2,1)S(1)}, u32[]{:S(2)}, u32[]{:S(2)}) collective-permute-start(bf16[1024,128]{1,0:T(8,128)(2,1)S(1)} %copy-done.12), channel_id=1, source_target_pairs={{0,0},{1,128},{2,64},{3,192},{64,1},{65,129},{66,65},{67,193},{128... | collective-permute-start | bytes 786440 | tf_op jit(solution)/shard_map/ppermute | solution.py:298
  12.2 16.8 %collective-permute-start.1 = (bf16[1024,128]{1,0:T(8,128)(2,1)S(1)}, bf16[1024,128]{1,0:T(8,128)(2,1)S(1)}, u32[]{:S(2)}, u32[]{:S(2)}) collective-permute-start(bf16[1024,128]{1,0:T(8,128)(2,1)S(1)} %copy-done.12), channel_id=1, source_target_pairs={{0,128},{1,0},{2,192},{3,64},{64,129},{65,1},{66,193},{67,65},{128... | collective-permute-start | bytes 786440 | tf_op jit(solution)/shard_map/ppermute | solution.py:298
  29.1 16.4 %collective-permute-start.7 = (bf16[512,1024]{1,0:T(8,128)(2,1)}, bf16[512,1024]{1,0:T(8,128)(2,1)}, u32[]{:S(2)}, u32[]{:S(2)}) collective-permute-start(bf16[512,1024]{1,0:T(8,128)(2,1)} %shard_map.83.refs_0_), channel_id=1, source_target_pairs={{0,2},{1,35},{2,32},{3,1},{32,34},{33,3},{34,0},{35,33},{4,6},{5,3... | collective-permute-start | bytes 3145736 | tf_op jit(solution)/shard_map/ppermute | solution.py:292
  31.1 10.6 %collective-permute-start.3 = (bf16[2048,128]{1,0:T(8,128)(2,1)S(1)}, bf16[2048,128]{1,0:T(8,128)(2,1)S(1)}, u32[]{:S(2)}, u32[]{:S(2)}) collective-permute-start(bf16[2048,128]{1,0:T(8,128)(2,1)S(1)} %constant_dynamic-update-slice_fusion.refs_8_), channel_id=1, source_target_pairs={{0,28},{4,0},{8,4},{12,8},{16,12},{20,16},{24,20},{28,24},{1,29},{... | collective-permute-start | bytes 1572872 | tf_op jit(solution)/shard_map/ppermute | solution.py:287
  31.7 12.1 %collective-permute-start.4 = (bf16[2048,128]{1,0:T(8,128)(2,1)S(1)}, bf16[2048,128]{1,0:T(8,128)(2,1)S(1)}, u32[]{:S(2)}, u32[]{:S(2)}) collective-permute-start(bf16[2048,128]{1,0:T(8,128)(2,1)S(1)} %constant_dynamic-update-slice_fusion.refs_8_), channel_id=1, source_target_pairs={{0,4},{4,8},{8,12},{12,16},{16,20},{20,24},{24,28},{28,0},{1,5},{5... | collective-permute-start | bytes 1572872 | tf_op jit(solution)/shard_map/ppermute | solution.py:287
  45.5 15.4 %collective-permute-start.12 = (bf16[512,1024]{1,0:T(8,128)(2,1)}, bf16[512,1024]{1,0:T(8,128)(2,1)}, u32[]{:S(2)}, u32[]{:S(2)}) collective-permute-start(bf16[512,1024]{1,0:T(8,128)(2,1)} %shard_map.83.refs_0_), channel_id=1, source_target_pairs={{0,34},{1,3},{2,0},{3,33},{32,2},{33,35},{34,32},{35,1},{4,38},{5,... | collective-permute-start | bytes 3145736 | tf_op jit(solution)/shard_map/ppermute | solution.py:292
  47.0 10.4 %collective-permute-start.10 = (bf16[2048,128]{1,0:T(8,128)(2,1)S(1)}, bf16[2048,128]{1,0:T(8,128)(2,1)S(1)}, u32[]{:S(2)}, u32[]{:S(2)}) collective-permute-start(bf16[2048,128]{1,0:T(8,128)(2,1)S(1)} %pad_maximum_fusion.1), channel_id=1, source_target_pairs={{0,192},{64,0},{128,64},{192,128},{1,193},{65,1},{129,65},{193,129... | collective-permute-start | bytes 1572872 | tf_op jit(solution)/shard_map/ppermute | solution.py:287
  47.9 10.5 %collective-permute-start.11 = (bf16[2048,128]{1,0:T(8,128)(2,1)S(1)}, bf16[2048,128]{1,0:T(8,128)(2,1)S(1)}, u32[]{:S(2)}, u32[]{:S(2)}) collective-permute-start(bf16[2048,128]{1,0:T(8,128)(2,1)S(1)} %pad_maximum_fusion.1), channel_id=1, source_target_pairs={{0,64},{64,128},{128,192},{192,0},{1,65},{65,129},{129,193},{193,1... | collective-permute-start | bytes 1572872 | tf_op jit(solution)/shard_map/ppermute | solution.py:287
  48.6 9.8 %collective-permute-start.8 = (bf16[2048,128]{1,0:T(8,128)(2,1)S(1)}, bf16[2048,128]{1,0:T(8,128)(2,1)S(1)}, u32[]{:S(2)}, u32[]{:S(2)}) collective-permute-start(bf16[2048,128]{1,0:T(8,128)(2,1)S(1)} %collective-permute-done.3.refs_11_), channel_id=1, source_target_pairs={{0,28},{4,0},{8,4},{12,8},{16,12},{20,16},{24,20},{28,24},{1,29},{... | collective-permute-start | bytes 1572872 | tf_op jit(solution)/shard_map/ppermute | solution.py:287
  48.6 10.8 %collective-permute-start.9 = (bf16[2048,128]{1,0:T(8,128)(2,1)S(1)}, bf16[2048,128]{1,0:T(8,128)(2,1)S(1)}, u32[]{:S(2)}, u32[]{:S(2)}) collective-permute-start(bf16[2048,128]{1,0:T(8,128)(2,1)S(1)} %collective-permute-done.4.refs_14_), channel_id=1, source_target_pairs={{0,4},{4,8},{8,12},{12,16},{16,20},{20,24},{24,28},{28,0},{1,5},{5... | collective-permute-start | bytes 1572872 | tf_op jit(solution)/shard_map/ppermute | solution.py:287
  60.9 17.7 %collective-permute-start.17 = (bf16[512,1024]{1,0:T(8,128)(2,1)}, bf16[512,1024]{1,0:T(8,128)(2,1)}, u32[]{:S(2)}, u32[]{:S(2)}) collective-permute-start(bf16[512,1024]{1,0:T(8,128)(2,1)} %collective-permute-done.7.refs_1_), channel_id=1, source_target_pairs={{0,2},{1,35},{2,32},{3,1},{32,34},{33,3},{34,0},{35,33},{4,6},{5,3... | collective-permute-start | bytes 3145736 | tf_op jit(solution)/shard_map/ppermute | solution.py:292
  62.8 11.6 %collective-permute-start.15 = (bf16[2048,128]{1,0:T(8,128)(2,1)S(1)}, bf16[2048,128]{1,0:T(8,128)(2,1)S(1)}, u32[]{:S(2)}, u32[]{:S(2)}) collective-permute-start(bf16[2048,128]{1,0:T(8,128)(2,1)S(1)} %pad_maximum_fusion.2), channel_id=1, source_target_pairs={{0,192},{64,0},{128,64},{192,128},{1,193},{65,1},{129,65},{193,129... | collective-permute-start | bytes 1572872 | tf_op jit(solution)/shard_map/ppermute | solution.py:287
  64.8 11.1 %collective-permute-start.16 = (bf16[2048,128]{1,0:T(8,128)(2,1)S(1)}, bf16[2048,128]{1,0:T(8,128)(2,1)S(1)}, u32[]{:S(2)}, u32[]{:S(2)}) collective-permute-start(bf16[2048,128]{1,0:T(8,128)(2,1)S(1)} %pad_maximum_fusion.2), channel_id=1, source_target_pairs={{0,64},{64,128},{128,192},{192,0},{1,65},{65,129},{129,193},{193,1... | collective-permute-start | bytes 1572872 | tf_op jit(solution)/shard_map/ppermute | solution.py:287
  64.9 11.0 %collective-permute-start.13 = (bf16[2048,128]{1,0:T(8,128)(2,1)S(1)}, bf16[2048,128]{1,0:T(8,128)(2,1)S(1)}, u32[]{:S(2)}, u32[]{:S(2)}) collective-permute-start(bf16[2048,128]{1,0:T(8,128)(2,1)S(1)} %collective-permute-done.8.refs_15_), channel_id=1, source_target_pairs={{0,28},{4,0},{8,4},{12,8},{16,12},{20,16},{24,20},{28,24},{1,29},{... | collective-permute-start | bytes 1572872 | tf_op jit(solution)/shard_map/ppermute | solution.py:287
  65.3 13.2 %collective-permute-start.14 = (bf16[2048,128]{1,0:T(8,128)(2,1)S(1)}, bf16[2048,128]{1,0:T(8,128)(2,1)S(1)}, u32[]{:S(2)}, u32[]{:S(2)}) collective-permute-start(bf16[2048,128]{1,0:T(8,128)(2,1)S(1)} %collective-permute-done.9.refs_18_), channel_id=1, source_target_pairs={{0,4},{4,8},{8,12},{12,16},{16,20},{20,24},{24,28},{28,0},{1,5},{5... | collective-permute-start | bytes 1572872 | tf_op jit(solution)/shard_map/ppermute | solution.py:287
  82.7 24.1 %collective-permute-start.19 = (bf16[2048,128]{1,0:T(8,128)(2,1)S(1)}, bf16[2048,128]{1,0:T(8,128)(2,1)S(1)}, u32[]{:S(2)}, u32[]{:S(2)}) collective-permute-start(bf16[2048,128]{1,0:T(8,128)(2,1)S(1)} %pad_maximum_fusion.3), channel_id=1, source_target_pairs={{0,192},{64,0},{128,64},{192,128},{1,193},{65,1},{129,65},{193,129... | collective-permute-start | bytes 1572872 | tf_op jit(solution)/shard_map/ppermute | solution.py:287
  84.5 22.2 %collective-permute-start.20 = (bf16[2048,128]{1,0:T(8,128)(2,1)S(1)}, bf16[2048,128]{1,0:T(8,128)(2,1)S(1)}, u32[]{:S(2)}, u32[]{:S(2)}) collective-permute-start(bf16[2048,128]{1,0:T(8,128)(2,1)S(1)} %pad_maximum_fusion.3), channel_id=1, source_target_pairs={{0,64},{64,128},{128,192},{192,0},{1,65},{65,129},{129,193},{193,1... | collective-permute-start | bytes 1572872 | tf_op jit(solution)/shard_map/ppermute | solution.py:287
  86.0 20.8 %collective-permute-start.18 = (bf16[2048,128]{1,0:T(8,128)(2,1)S(1)}, bf16[2048,128]{1,0:T(8,128)(2,1)S(1)}, u32[]{:S(2)}, u32[]{:S(2)}) collective-permute-start(bf16[2048,128]{1,0:T(8,128)(2,1)S(1)} %collective-permute-done.13.refs_1_), channel_id=1, source_target_pairs={{0,28},{4,0},{8,4},{12,8},{16,12},{20,16},{24,20},{28,24},{1,29},{... | collective-permute-start | bytes 1572872 | tf_op jit(solution)/shard_map/ppermute | solution.py:287
  108.4 17.5 %collective-permute-start.25 = (bf16[2,128,640]{2,1,0:T(8,128)(2,1)}, bf16[2,128,640]{2,1,0:T(8,128)(2,1)S(1)}, u32[]{:S(2)}, u32[]{:S(2)}) collective-permute-start(bf16[2,128,640]{2,1,0:T(8,128)(2,1)} %get-tuple-element.73), channel_id=1, source_target_pairs={{0,2},{2,32},{32,34},{34,0},{1,3},{3,33},{33,35},{35,1},{4,6},{6,3... | collective-permute-start | bytes 983048 | tf_op jit(solution)/shard_map/ppermute | solution.py:287
  108.4 17.5 %collective-permute-start.26 = (bf16[2,128,640]{2,1,0:T(8,128)(2,1)}, bf16[2,128,640]{2,1,0:T(8,128)(2,1)S(1)}, u32[]{:S(2)}, u32[]{:S(2)}) collective-permute-start(bf16[2,128,640]{2,1,0:T(8,128)(2,1)} %get-tuple-element.74), channel_id=1, source_target_pairs={{0,32},{2,34},{32,0},{34,2},{1,33},{3,35},{33,1},{35,3},{4,36},{6,... | collective-permute-start | bytes 983048 | tf_op jit(solution)/shard_map/ppermute | solution.py:287
  110.8 15.4 %collective-permute-start.27 = (bf16[2,128,640]{2,1,0:T(8,128)(2,1)}, bf16[2,128,640]{2,1,0:T(8,128)(2,1)S(1)}, u32[]{:S(2)}, u32[]{:S(2)}) collective-permute-start(bf16[2,128,640]{2,1,0:T(8,128)(2,1)} %get-tuple-element.75), channel_id=1, source_target_pairs={{0,34},{2,0},{32,2},{34,32},{1,35},{3,1},{33,3},{35,33},{4,38},{6,... | collective-permute-start | bytes 983048 | tf_op jit(solution)/shard_map/ppermute | solution.py:287
  121.4 16.9 %all-to-all-start = ((bf16[8,128,384]{2,1,0:T(8,128)(2,1)}), bf16[8,128,384]{2,1,0:T(8,128)(2,1)S(1)}, u32[]{:S(2)}, u32[]{:S(2)}) async-start(bf16[8,128,384]{2,1,0:T(8,128)(2,1)} %shard_map.86), calls=%async_computation | async-start | bytes 1572864 | tf_op jit(solution)/shard_map/all_to_all | solution.py:385
  127.2 11.1 %collective-permute-start.28 = (bf16[4,128,640]{2,1,0:T(8,128)(2,1)}, bf16[4,128,640]{2,1,0:T(8,128)(2,1)S(1)}, u32[]{:S(2)}, u32[]{:S(2)}) collective-permute-start(bf16[4,128,640]{2,1,0:T(8,128)(2,1)} %pad_maximum_fusion), channel_id=1, source_target_pairs={{0,1},{1,0},{2,3},{3,2},{4,5},{5,4},{6,7},{7,6},{8,9},{9,8},{10,11... | collective-permute-start | bytes 1966088 | tf_op jit(solution)/shard_map/ppermute | solution.py:302
  (23 other events, 387.5 us)
